TPU v7x, 256 devices: a whole 4x4x8 slice. The times are simulated.
256 devices in a mesh: vel: 16 (over z, x_hi), cell: 16 (over x_lo, y, core).
Axes of the slice: x: 4 (x_hi: 2, x_lo: 2; x = x_hi * 2 + x_lo), y: 4, z: 8, core: 2. Of those that a mesh axis runs over, the one named last changes fastest.
Arguments:
- distribution: float32 [13824, 2048], P('vel', 'cell'), may hold values from 0.2 to 2
- pair_first: int32 [16, 16, 256], P('vel'), may hold values from 0 to 863
- pair_second: int32 [16, 16, 256], P('vel'), may hold values from 0 to 863
- pair_weight: float32 [16, 16, 256], P('vel'), may hold values from 0.05 to 0.5
- proj_pair: int32 [16, 16, 16, 64], P('vel'), may hold values from 0 to 255
- proj_target: int32 [16, 16, 16, 64], P(None, None, 'vel'), may hold values from 0 to 863
- proj_coef: float32 [16, 16, 16, 64], P(None, None, 'vel'), may hold values from 0.1 to 1
- slot_counts: int32 [16, 16, 16], P(None, None, 'vel'), may hold values from 16 to 64, as said below
Outputs:
- transported: float32 [13824, 2048], P('vel', 'cell')
- collision: float32 [13824, 2048], P('vel', 'cell')
Inputs may be any that keep to these rules, and one draw needn't show every extreme that they name: slot_counts[s, p, o] live slots, counted from the first, in the list that source group s fills for partner group p and owner group o; for every offset (s - p) mod 16 one owner group gets exactly 64 live slots from every source group.
All inputs are finite; a program needn't handle non-finite values.
Results may differ from a plain program's by a relative error of at most 0.000054.
Values sent between devices are 32-bit elements; how exact they have to be, the bound alone decides.
A program may use at most 64 MiB of HBM per device.

v0:
```python
import jax
import jax.numpy as jnp
from jax import lax
from jax.sharding import PartitionSpec as P

VSIDE = 24


def with_halo(cells, sides, width):
    for axis, dim in sides:
        count = lax.axis_size(axis)
        head = lax.slice_in_dim(cells, 0, width, axis=dim)
        tail = lax.slice_in_dim(cells, cells.shape[dim] - width, cells.shape[dim], axis=dim)
        cells = jnp.concatenate(
            [
                lax.ppermute(tail, axis, [(i, (i + 1) % count) for i in range(count)]),
                cells,
                lax.ppermute(head, axis, [((i + 1) % count, i) for i in range(count)]),
            ],
            axis=dim,
        )
    return cells


def shifted(value, axis, steps):
    count = lax.axis_size(axis)
    pairs = [(source, (source + steps) % count) for source in range(count)]
    return lax.ppermute(value, axis, pairs)


def on_device(
    distribution,
    pair_first,
    pair_second,
    pair_weight,
    proj_pair,
    proj_target,
    proj_coef,
    slot_counts,
):
    block_rows, cell_count = distribution.shape
    groups = lax.axis_size("vel")
    position = lax.axis_index("vel")
    slot_count = proj_target.shape[3]
    own_rows = jnp.arange(block_rows, dtype=jnp.int32)
    first_axis = (position * block_rows + own_rows) // (VSIDE * VSIDE)
    courant = ((2 * first_axis - VSIDE + 1) / (2.0 * VSIDE)).astype(jnp.float32)[:, None]
    padded = with_halo(distribution, (("cell", 1),), 1)
    transported = (
        distribution
        - jnp.maximum(courant, 0.0) * (distribution - padded[:, :-2])
        - jnp.minimum(courant, 0.0) * (padded[:, 2:] - distribution)
    )
    live_mask = (
        jnp.arange(slot_count, dtype=jnp.int32)[None, None, None, :] < slot_counts[:, :, :, None]
    )
    weights_live = jnp.where(live_mask, proj_coef, 0.0)[:, :, 0, :]
    target_rows = proj_target[:, :, 0, :]

    def pair_terms(arrived, partner):
        first_rows = pair_first[0, partner]
        second_values = arrived[pair_second[0, partner]]
        product = pair_weight[0, partner][:, None] * transported[first_rows] * second_values
        one_hot = (own_rows[:, None] == first_rows[None, :]).astype(jnp.float32)
        loss_part = jnp.dot(
            one_hot, product, precision=lax.Precision.HIGHEST, preferred_element_type=jnp.float32
        )
        outgoing = product[proj_pair[0, partner]]
        return (loss_part, outgoing)

    def take_gain(received, targets_flat, factors_flat):
        one_hot = jnp.where(own_rows[:, None] == targets_flat[None, :], factors_flat[None, :], 0.0)
        return jnp.dot(
            one_hot, received, precision=lax.Precision.HIGHEST, preferred_element_type=jnp.float32
        )

    def handle(status, arrived, offset, picked=False):
        loss_sum, gain_sum, stored = status
        partner = (position - offset) % groups
        loss_part, outgoing = pair_terms(arrived, partner)
        loss_sum = loss_sum + loss_part
        received = lax.all_to_all(outgoing, "vel", split_axis=0, concat_axis=0, tiled=True)
        sources = jnp.arange(groups, dtype=jnp.int32)
        from_partner = (sources - offset) % groups
        factors = weights_live[sources, from_partner].reshape(-1)
        targets = target_rows[sources, from_partner].reshape(-1)
        gain_sum = gain_sum + take_gain(received.reshape(-1, cell_count), targets, factors)
        return (loss_sum, gain_sum, stored)

    stored = jnp.zeros((1,), jnp.float32)
    empty = jnp.zeros((block_rows, cell_count), jnp.float32)
    status = (empty, empty, stored)
    status = handle(status, transported, 0)

    def advance(offset, carried):
        arrived, partial_value = carried
        arrived = shifted(arrived, "vel", 1)
        return (arrived, handle(partial_value, arrived, offset))

    arrived, status = lax.fori_loop(1, groups, advance, (transported, status))
    loss_sum, gain_sum, stored = status
    return (transported, gain_sum - loss_sum)


def solution(mesh):
    in_specs = (
        P("vel", "cell"),
        P("vel", None, None),
        P("vel", None, None),
        P("vel", None, None),
        P("vel", None, None, None),
        P(None, None, "vel", None),
        P(None, None, "vel", None),
        P(None, None, "vel"),
    )
    out_specs = (P("vel", "cell"), P("vel", "cell"))
    return jax.shard_map(
        on_device, mesh=mesh, in_specs=in_specs, out_specs=out_specs, check_vma=False
    )
```

profile of v0, /device:TPU:16, one launch (start us, length us, event | category | flops | bytes accessed | tf_op | source)
XLA Modules:
  0.0 662.8 jit_solution(6672785300760412288)
XLA Ops:
  12.1 4.0 gather_fusion.9
  16.1 11.2 %all-to-all-start.1 = ((f32[16,64,128]{2,1,0:T(8,128)}), f32[16,64,128]{2,1,0:T(8,128)S(1)}, u32[]{:S(2)}, u32[]{:S(2)}) async-start(f32[16,64,128]{2,1,0:T(8,128)} %bitcast.12), calls=%async_computation.1 | async-start | bytes 1048576 | tf_op jit(solution)/shard_map/all_to_all | solution.py:82
  29.4 17.4 %all-to-all-done.1 = f32[16,64,128]{2,1,0:T(8,128)S(1)} async-done(((f32[16,64,128]{2,1,0:T(8,128)}), f32[16,64,128]{2,1,0:T(8,128)S(1)}, u32[]{:S(2)}, u32[]{:S(2)}) %all-to-all-start.1) | async-done | bytes 524320 | tf_op jit(solution)/shard_map/all_to_all | solution.py:82
  49.7 612.1 %while.21 = (s32[]{:T(128)}, f32[864,128]{1,0:T(8,128)S(1)}, f32[864,128]{1,0:T(8,128)S(1)}, f32[864,128]{1,0:T(8,128)S(1)}, s32[]{:T(128)}, /*index=5*/s32[1,16...) while((s32[]{:T(128)}, f32[864,128]{1,0:T(8,128)S(1)}, ...), condition=%wide.region_1.2_spmd.clone.clone, body=%wide.region_0.1_spmd.clone.clone.sunk | while | flops 1700978432 | bytes 8709832 | solution.py:100
  52.9 13.6 %collective-permute-done = f32[864,128]{1,0:T(8,128)S(1)} collective-permute-done((f32[864,128]{1,0:T(8,128)S(1)}, f32[864,128]{1,0:T(8,128)S(1)}, u32[]{:S(2)}, u32[]{:S(2)}) %collective-permute-start) | collective-permute-done | bytes 442400 | tf_op jit(solution)/shard_map/while/body/eval_jaxpr/ppermute | solution.py:28
  67.3 4.0 gather_fusion.2
  76.9 17.9 %all-to-all-done = f32[16,64,128]{2,1,0:T(8,128)S(1)} async-done(((f32[16,64,128]{2,1,0:T(8,128)}), f32[16,64,128]{2,1,0:T(8,128)S(1)}, u32[]{:S(2)}, u32[]{:S(2)}) %all-to-all-start) | async-done | bytes 524320 | tf_op jit(solution)/shard_map/while/body/eval_jaxpr/all_to_all | solution.py:82
  101.5 10.0 %collective-permute-done = f32[864,128]{1,0:T(8,128)S(1)} collective-permute-done((f32[864,128]{1,0:T(8,128)S(1)}, f32[864,128]{1,0:T(8,128)S(1)}, u32[]{:S(2)}, u32[]{:S(2)}) %collective-permute-start) | collective-permute-done | bytes 442400 | tf_op jit(solution)/shard_map/while/body/eval_jaxpr/ppermute | solution.py:28
  112.4 4.0 gather_fusion.2
  116.4 4.1 all-to-all-start
  122.6 16.0 %all-to-all-done = f32[16,64,128]{2,1,0:T(8,128)S(1)} async-done(((f32[16,64,128]{2,1,0:T(8,128)}), f32[16,64,128]{2,1,0:T(8,128)S(1)}, u32[]{:S(2)}, u32[]{:S(2)}) %all-to-all-start) | async-done | bytes 524320 | tf_op jit(solution)/shard_map/while/body/eval_jaxpr/all_to_all | solution.py:82
  144.8 9.3 %collective-permute-done = f32[864,128]{1,0:T(8,128)S(1)} collective-permute-done((f32[864,128]{1,0:T(8,128)S(1)}, f32[864,128]{1,0:T(8,128)S(1)}, u32[]{:S(2)}, u32[]{:S(2)}) %collective-permute-start) | collective-permute-done | bytes 442400 | tf_op jit(solution)/shard_map/while/body/eval_jaxpr/ppermute | solution.py:28
  155.0 4.0 gather_fusion.2
  164.9 14.2 %all-to-all-done = f32[16,64,128]{2,1,0:T(8,128)S(1)} async-done(((f32[16,64,128]{2,1,0:T(8,128)}), f32[16,64,128]{2,1,0:T(8,128)S(1)}, u32[]{:S(2)}, u32[]{:S(2)}) %all-to-all-start) | async-done | bytes 524320 | tf_op jit(solution)/shard_map/while/body/eval_jaxpr/all_to_all | solution.py:82
  185.8 8.4 %collective-permute-done = f32[864,128]{1,0:T(8,128)S(1)} collective-permute-done((f32[864,128]{1,0:T(8,128)S(1)}, f32[864,128]{1,0:T(8,128)S(1)}, u32[]{:S(2)}, u32[]{:S(2)}) %collective-permute-start) | collective-permute-done | bytes 442400 | tf_op jit(solution)/shard_map/while/body/eval_jaxpr/ppermute | solution.py:28
  195.0 4.0 gather_fusion.2
  204.7 12.6 %all-to-all-done = f32[16,64,128]{2,1,0:T(8,128)S(1)} async-done(((f32[16,64,128]{2,1,0:T(8,128)}), f32[16,64,128]{2,1,0:T(8,128)S(1)}, u32[]{:S(2)}, u32[]{:S(2)}) %all-to-all-start) | async-done | bytes 524320 | tf_op jit(solution)/shard_map/while/body/eval_jaxpr/all_to_all | solution.py:82
  223.8 8.6 %collective-permute-done = f32[864,128]{1,0:T(8,128)S(1)} collective-permute-done((f32[864,128]{1,0:T(8,128)S(1)}, f32[864,128]{1,0:T(8,128)S(1)}, u32[]{:S(2)}, u32[]{:S(2)}) %collective-permute-start) | collective-permute-done | bytes 442400 | tf_op jit(solution)/shard_map/while/body/eval_jaxpr/ppermute | solution.py:28
  233.2 4.0 gather_fusion.2
  242.8 12.5 %all-to-all-done = f32[16,64,128]{2,1,0:T(8,128)S(1)} async-done(((f32[16,64,128]{2,1,0:T(8,128)}), f32[16,64,128]{2,1,0:T(8,128)S(1)}, u32[]{:S(2)}, u32[]{:S(2)}) %all-to-all-start) | async-done | bytes 524320 | tf_op jit(solution)/shard_map/while/body/eval_jaxpr/all_to_all | solution.py:82
  262.0 8.4 %collective-permute-done = f32[864,128]{1,0:T(8,128)S(1)} collective-permute-done((f32[864,128]{1,0:T(8,128)S(1)}, f32[864,128]{1,0:T(8,128)S(1)}, u32[]{:S(2)}, u32[]{:S(2)}) %collective-permute-start) | collective-permute-done | bytes 442400 | tf_op jit(solution)/shard_map/while/body/eval_jaxpr/ppermute | solution.py:28
  271.3 4.0 gather_fusion.2
  280.9 13.9 %all-to-all-done = f32[16,64,128]{2,1,0:T(8,128)S(1)} async-done(((f32[16,64,128]{2,1,0:T(8,128)}), f32[16,64,128]{2,1,0:T(8,128)S(1)}, u32[]{:S(2)}, u32[]{:S(2)}) %all-to-all-start) | async-done | bytes 524320 | tf_op jit(solution)/shard_map/while/body/eval_jaxpr/all_to_all | solution.py:82
  301.0 8.9 %collective-permute-done = f32[864,128]{1,0:T(8,128)S(1)} collective-permute-done((f32[864,128]{1,0:T(8,128)S(1)}, f32[864,128]{1,0:T(8,128)S(1)}, u32[]{:S(2)}, u32[]{:S(2)}) %collective-permute-start) | collective-permute-done | bytes 442400 | tf_op jit(solution)/shard_map/while/body/eval_jaxpr/ppermute | solution.py:28
  310.8 4.0 gather_fusion.2
  320.4 15.5 %all-to-all-done = f32[16,64,128]{2,1,0:T(8,128)S(1)} async-done(((f32[16,64,128]{2,1,0:T(8,128)}), f32[16,64,128]{2,1,0:T(8,128)S(1)}, u32[]{:S(2)}, u32[]{:S(2)}) %all-to-all-start) | async-done | bytes 524320 | tf_op jit(solution)/shard_map/while/body/eval_jaxpr/all_to_all | solution.py:82
  342.2 9.0 %collective-permute-done = f32[864,128]{1,0:T(8,128)S(1)} collective-permute-done((f32[864,128]{1,0:T(8,128)S(1)}, f32[864,128]{1,0:T(8,128)S(1)}, u32[]{:S(2)}, u32[]{:S(2)}) %collective-permute-start) | collective-permute-done | bytes 442400 | tf_op jit(solution)/shard_map/while/body/eval_jaxpr/ppermute | solution.py:28
  352.0 4.0 gather_fusion.2
  361.7 15.5 %all-to-all-done = f32[16,64,128]{2,1,0:T(8,128)S(1)} async-done(((f32[16,64,128]{2,1,0:T(8,128)}), f32[16,64,128]{2,1,0:T(8,128)S(1)}, u32[]{:S(2)}, u32[]{:S(2)}) %all-to-all-start) | async-done | bytes 524320 | tf_op jit(solution)/shard_map/while/body/eval_jaxpr/all_to_all | solution.py:82
  383.4 9.2 %collective-permute-done = f32[864,128]{1,0:T(8,128)S(1)} collective-permute-done((f32[864,128]{1,0:T(8,128)S(1)}, f32[864,128]{1,0:T(8,128)S(1)}, u32[]{:S(2)}, u32[]{:S(2)}) %collective-permute-start) | collective-permute-done | bytes 442400 | tf_op jit(solution)/shard_map/while/body/eval_jaxpr/ppermute | solution.py:28
  393.4 4.0 gather_fusion.2
  403.1 13.9 %all-to-all-done = f32[16,64,128]{2,1,0:T(8,128)S(1)} async-done(((f32[16,64,128]{2,1,0:T(8,128)}), f32[16,64,128]{2,1,0:T(8,128)S(1)}, u32[]{:S(2)}, u32[]{:S(2)}) %all-to-all-start) | async-done | bytes 524320 | tf_op jit(solution)/shard_map/while/body/eval_jaxpr/all_to_all | solution.py:82
  423.2 9.0 %collective-permute-done = f32[864,128]{1,0:T(8,128)S(1)} collective-permute-done((f32[864,128]{1,0:T(8,128)S(1)}, f32[864,128]{1,0:T(8,128)S(1)}, u32[]{:S(2)}, u32[]{:S(2)}) %collective-permute-start) | collective-permute-done | bytes 442400 | tf_op jit(solution)/shard_map/while/body/eval_jaxpr/ppermute | solution.py:28
  433.0 4.0 gather_fusion.2
  442.7 15.6 %all-to-all-done = f32[16,64,128]{2,1,0:T(8,128)S(1)} async-done(((f32[16,64,128]{2,1,0:T(8,128)}), f32[16,64,128]{2,1,0:T(8,128)S(1)}, u32[]{:S(2)}, u32[]{:S(2)}) %all-to-all-start) | async-done | bytes 524320 | tf_op jit(solution)/shard_map/while/body/eval_jaxpr/all_to_all | solution.py:82
  464.5 9.0 %collective-permute-done = f32[864,128]{1,0:T(8,128)S(1)} collective-permute-done((f32[864,128]{1,0:T(8,128)S(1)}, f32[864,128]{1,0:T(8,128)S(1)}, u32[]{:S(2)}, u32[]{:S(2)}) %collective-permute-start) | collective-permute-done | bytes 442400 | tf_op jit(solution)/shard_map/while/body/eval_jaxpr/ppermute | solution.py:28
  474.4 4.0 gather_fusion.2
  484.0 15.1 %all-to-all-done = f32[16,64,128]{2,1,0:T(8,128)S(1)} async-done(((f32[16,64,128]{2,1,0:T(8,128)}), f32[16,64,128]{2,1,0:T(8,128)S(1)}, u32[]{:S(2)}, u32[]{:S(2)}) %all-to-all-start) | async-done | bytes 524320 | tf_op jit(solution)/shard_map/while/body/eval_jaxpr/all_to_all | solution.py:82
  505.4 9.0 %collective-permute-done = f32[864,128]{1,0:T(8,128)S(1)} collective-permute-done((f32[864,128]{1,0:T(8,128)S(1)}, f32[864,128]{1,0:T(8,128)S(1)}, u32[]{:S(2)}, u32[]{:S(2)}) %collective-permute-start) | collective-permute-done | bytes 442400 | tf_op jit(solution)/shard_map/while/body/eval_jaxpr/ppermute | solution.py:28
  515.2 4.0 gather_fusion.2
  524.9 14.5 %all-to-all-done = f32[16,64,128]{2,1,0:T(8,128)S(1)} async-done(((f32[16,64,128]{2,1,0:T(8,128)}), f32[16,64,128]{2,1,0:T(8,128)S(1)}, u32[]{:S(2)}, u32[]{:S(2)}) %all-to-all-start) | async-done | bytes 524320 | tf_op jit(solution)/shard_map/while/body/eval_jaxpr/all_to_all | solution.py:82
  545.6 9.0 %collective-permute-done = f32[864,128]{1,0:T(8,128)S(1)} collective-permute-done((f32[864,128]{1,0:T(8,128)S(1)}, f32[864,128]{1,0:T(8,128)S(1)}, u32[]{:S(2)}, u32[]{:S(2)}) %collective-permute-start) | collective-permute-done | bytes 442400 | tf_op jit(solution)/shard_map/while/body/eval_jaxpr/ppermute | solution.py:28
  555.4 4.0 gather_fusion.2
  565.1 15.6 %all-to-all-done = f32[16,64,128]{2,1,0:T(8,128)S(1)} async-done(((f32[16,64,128]{2,1,0:T(8,128)}), f32[16,64,128]{2,1,0:T(8,128)S(1)}, u32[]{:S(2)}, u32[]{:S(2)}) %all-to-all-start) | async-done | bytes 524320 | tf_op jit(solution)/shard_map/while/body/eval_jaxpr/all_to_all | solution.py:82
  586.9 9.1 %collective-permute-done = f32[864,128]{1,0:T(8,128)S(1)} collective-permute-done((f32[864,128]{1,0:T(8,128)S(1)}, f32[864,128]{1,0:T(8,128)S(1)}, u32[]{:S(2)}, u32[]{:S(2)}) %collective-permute-start) | collective-permute-done | bytes 442400 | tf_op jit(solution)/shard_map/while/body/eval_jaxpr/ppermute | solution.py:28
  606.5 14.1 %all-to-all-done = f32[16,64,128]{2,1,0:T(8,128)S(1)} async-done(((f32[16,64,128]{2,1,0:T(8,128)}), f32[16,64,128]{2,1,0:T(8,128)S(1)}, u32[]{:S(2)}, u32[]{:S(2)}) %all-to-all-start) | async-done | bytes 524320 | tf_op jit(solution)/shard_map/while/body/eval_jaxpr/all_to_all | solution.py:82
  626.8 9.0 %collective-permute-done = f32[864,128]{1,0:T(8,128)S(1)} collective-permute-done((f32[864,128]{1,0:T(8,128)S(1)}, f32[864,128]{1,0:T(8,128)S(1)}, u32[]{:S(2)}, u32[]{:S(2)}) %collective-permute-start) | collective-permute-done | bytes 442400 | tf_op jit(solution)/shard_map/while/body/eval_jaxpr/ppermute | solution.py:28
  646.3 12.4 %all-to-all-done = f32[16,64,128]{2,1,0:T(8,128)S(1)} async-done(((f32[16,64,128]{2,1,0:T(8,128)}), f32[16,64,128]{2,1,0:T(8,128)S(1)}, u32[]{:S(2)}, u32[]{:S(2)}) %all-to-all-start) | async-done | bytes 524320 | tf_op jit(solution)/shard_map/while/body/eval_jaxpr/all_to_all | solution.py:82
  (338 shorter events, 212.8 us)
Async XLA Ops:
  0.6 9.2 %copy-start.1 = (f32[864,128]{1,0:T(8,128)S(1)}, f32[864,128]{1,0:T(8,128)}, u32[]{:S(2)}) copy-start(f32[864,128]{1,0:T(8,128)} %param.10) | copy-start | bytes 1327108
  2.0 7.8 %collective-permute-start.1 = (f32[864,1]{1,0:T(8,128)S(1)}, f32[864,1]{1,0:T(8,128)S(1)}, u32[]{:S(2)}, u32[]{:S(2)}) collective-permute-start(f32[864,1]{1,0:T(8,128)S(1)} %get-tuple-element.402), channel_id=1, source_target_pairs={{0,1},{1,2},{2,3},{3,4},{4,5},{5,6},{6,7},{7,8},{8,9},{9,10},{10,1... | collective-permute-start | bytes 10376 | tf_op jit(solution)/shard_map/ppermute | solution.py:16
  2.1 7.7 %collective-permute-start.2 = (f32[864,1]{1,0:T(8,128)S(1)}, f32[864,1]{1,0:T(8,128)S(1)}, u32[]{:S(2)}, u32[]{:S(2)}) collective-permute-start(f32[864,1]{1,0:T(8,128)S(1)} %get-tuple-element.403), channel_id=1, source_target_pairs={{1,0},{2,1},{3,2},{4,3},{5,4},{6,5},{7,6},{8,7},{9,8},{10,9},{11,1... | collective-permute-start | bytes 10376 | tf_op jit(solution)/shard_map/ppermute | solution.py:18
  16.1 11.2 %copy-start.2 = (s32[16,16,1,64]{3,2,1,0:T(1,128)S(1)}, s32[16,16,1,64]{3,2,1,0:T(1,128)}, u32[]{:S(2)}) copy-start(s32[16,16,1,64]{3,2,1,0:T(1,128)} %param.15) | copy-start | bytes 196612
  16.1 11.9 %copy-start.3 = (f32[16,16,1,64]{3,2,1,0:T(1,128)S(1)}, f32[16,16,1,64]{3,2,1,0:T(1,128)}, u32[]{:S(2)}) copy-start(f32[16,16,1,64]{3,2,1,0:T(1,128)} %param.16) | copy-start | bytes 196612
  16.1 11.9 %copy-start.4 = (s32[16,16,1]{1,2,0:T(1,128)S(1)}, s32[16,16,1]{1,2,0:T(1,128)}, u32[]{:S(2)}) copy-start(s32[16,16,1]{1,2,0:T(1,128)} %param.17) | copy-start | bytes 3076
  16.1 30.6 %all-to-all-start.1 = ((f32[16,64,128]{2,1,0:T(8,128)}), f32[16,64,128]{2,1,0:T(8,128)S(1)}, u32[]{:S(2)}, u32[]{:S(2)}) async-start(f32[16,64,128]{2,1,0:T(8,128)} %bitcast.12), calls=%async_computation.1 | async-start | bytes 1048576 | tf_op jit(solution)/shard_map/all_to_all | solution.py:82
  49.7 16.7 %collective-permute-start = (f32[864,128]{1,0:T(8,128)S(1)}, f32[864,128]{1,0:T(8,128)S(1)}, u32[]{:S(2)}, u32[]{:S(2)}) collective-permute-start(f32[864,128]{1,0:T(8,128)S(1)} %get-tuple-element.503), channel_id=1, source_target_pairs={{0,16},{16,32},{32,48},{48,64},{64,80},{80,96},{96,112},{112,128},... | collective-permute-start | bytes 1327112 | tf_op jit(solution)/shard_map/while/body/eval_jaxpr/ppermute | solution.py:28
  71.3 23.5 %all-to-all-start = ((f32[16,64,128]{2,1,0:T(8,128)}), f32[16,64,128]{2,1,0:T(8,128)S(1)}, u32[]{:S(2)}, u32[]{:S(2)}) async-start(f32[16,64,128]{2,1,0:T(8,128)} %bitcast.61), calls=%async_computation | async-start | bytes 1048576 | tf_op jit(solution)/shard_map/while/body/eval_jaxpr/all_to_all | solution.py:82
  97.9 13.6 %collective-permute-start = (f32[864,128]{1,0:T(8,128)S(1)}, f32[864,128]{1,0:T(8,128)S(1)}, u32[]{:S(2)}, u32[]{:S(2)}) collective-permute-start(f32[864,128]{1,0:T(8,128)S(1)} %get-tuple-element.503), channel_id=1, source_target_pairs={{0,16},{16,32},{32,48},{48,64},{64,80},{80,96},{96,112},{112,128},... | collective-permute-start | bytes 1327112 | tf_op jit(solution)/shard_map/while/body/eval_jaxpr/ppermute | solution.py:28
  116.4 22.2 %all-to-all-start = ((f32[16,64,128]{2,1,0:T(8,128)}), f32[16,64,128]{2,1,0:T(8,128)S(1)}, u32[]{:S(2)}, u32[]{:S(2)}) async-start(f32[16,64,128]{2,1,0:T(8,128)} %bitcast.61), calls=%async_computation | async-start | bytes 1048576 | tf_op jit(solution)/shard_map/while/body/eval_jaxpr/all_to_all | solution.py:82
  141.7 12.4 %collective-permute-start = (f32[864,128]{1,0:T(8,128)S(1)}, f32[864,128]{1,0:T(8,128)S(1)}, u32[]{:S(2)}, u32[]{:S(2)}) collective-permute-start(f32[864,128]{1,0:T(8,128)S(1)} %get-tuple-element.503), channel_id=1, source_target_pairs={{0,16},{16,32},{32,48},{48,64},{64,80},{80,96},{96,112},{112,128},... | collective-permute-start | bytes 1327112 | tf_op jit(solution)/shard_map/while/body/eval_jaxpr/ppermute | solution.py:28
  159.0 20.1 %all-to-all-start = ((f32[16,64,128]{2,1,0:T(8,128)}), f32[16,64,128]{2,1,0:T(8,128)S(1)}, u32[]{:S(2)}, u32[]{:S(2)}) async-start(f32[16,64,128]{2,1,0:T(8,128)} %bitcast.61), calls=%async_computation | async-start | bytes 1048576 | tf_op jit(solution)/shard_map/while/body/eval_jaxpr/all_to_all | solution.py:82
  182.2 12.0 %collective-permute-start = (f32[864,128]{1,0:T(8,128)S(1)}, f32[864,128]{1,0:T(8,128)S(1)}, u32[]{:S(2)}, u32[]{:S(2)}) collective-permute-start(f32[864,128]{1,0:T(8,128)S(1)} %get-tuple-element.503), channel_id=1, source_target_pairs={{0,16},{16,32},{32,48},{48,64},{64,80},{80,96},{96,112},{112,128},... | collective-permute-start | bytes 1327112 | tf_op jit(solution)/shard_map/while/body/eval_jaxpr/ppermute | solution.py:28
  199.1 18.2 %all-to-all-start = ((f32[16,64,128]{2,1,0:T(8,128)}), f32[16,64,128]{2,1,0:T(8,128)S(1)}, u32[]{:S(2)}, u32[]{:S(2)}) async-start(f32[16,64,128]{2,1,0:T(8,128)} %bitcast.61), calls=%async_computation | async-start | bytes 1048576 | tf_op jit(solution)/shard_map/while/body/eval_jaxpr/all_to_all | solution.py:82
  220.4 12.0 %collective-permute-start = (f32[864,128]{1,0:T(8,128)S(1)}, f32[864,128]{1,0:T(8,128)S(1)}, u32[]{:S(2)}, u32[]{:S(2)}) collective-permute-start(f32[864,128]{1,0:T(8,128)S(1)} %get-tuple-element.503), channel_id=1, source_target_pairs={{0,16},{16,32},{32,48},{48,64},{64,80},{80,96},{96,112},{112,128},... | collective-permute-start | bytes 1327112 | tf_op jit(solution)/shard_map/while/body/eval_jaxpr/ppermute | solution.py:28
  237.2 18.1 %all-to-all-start = ((f32[16,64,128]{2,1,0:T(8,128)}), f32[16,64,128]{2,1,0:T(8,128)S(1)}, u32[]{:S(2)}, u32[]{:S(2)}) async-start(f32[16,64,128]{2,1,0:T(8,128)} %bitcast.61), calls=%async_computation | async-start | bytes 1048576 | tf_op jit(solution)/shard_map/while/body/eval_jaxpr/all_to_all | solution.py:82
  258.4 12.0 %collective-permute-start = (f32[864,128]{1,0:T(8,128)S(1)}, f32[864,128]{1,0:T(8,128)S(1)}, u32[]{:S(2)}, u32[]{:S(2)}) collective-permute-start(f32[864,128]{1,0:T(8,128)S(1)} %get-tuple-element.503), channel_id=1, source_target_pairs={{0,16},{16,32},{32,48},{48,64},{64,80},{80,96},{96,112},{112,128},... | collective-permute-start | bytes 1327112 | tf_op jit(solution)/shard_map/while/body/eval_jaxpr/ppermute | solution.py:28
  275.3 19.5 %all-to-all-start = ((f32[16,64,128]{2,1,0:T(8,128)}), f32[16,64,128]{2,1,0:T(8,128)S(1)}, u32[]{:S(2)}, u32[]{:S(2)}) async-start(f32[16,64,128]{2,1,0:T(8,128)} %bitcast.61), calls=%async_computation | async-start | bytes 1048576 | tf_op jit(solution)/shard_map/while/body/eval_jaxpr/all_to_all | solution.py:82
  297.9 12.0 %collective-permute-start = (f32[864,128]{1,0:T(8,128)S(1)}, f32[864,128]{1,0:T(8,128)S(1)}, u32[]{:S(2)}, u32[]{:S(2)}) collective-permute-start(f32[864,128]{1,0:T(8,128)S(1)} %get-tuple-element.503), channel_id=1, source_target_pairs={{0,16},{16,32},{32,48},{48,64},{64,80},{80,96},{96,112},{112,128},... | collective-permute-start | bytes 1327112 | tf_op jit(solution)/shard_map/while/body/eval_jaxpr/ppermute | solution.py:28
  314.8 21.2 %all-to-all-start = ((f32[16,64,128]{2,1,0:T(8,128)}), f32[16,64,128]{2,1,0:T(8,128)S(1)}, u32[]{:S(2)}, u32[]{:S(2)}) async-start(f32[16,64,128]{2,1,0:T(8,128)} %bitcast.61), calls=%async_computation | async-start | bytes 1048576 | tf_op jit(solution)/shard_map/while/body/eval_jaxpr/all_to_all | solution.py:82
  339.1 12.1 %collective-permute-start = (f32[864,128]{1,0:T(8,128)S(1)}, f32[864,128]{1,0:T(8,128)S(1)}, u32[]{:S(2)}, u32[]{:S(2)}) collective-permute-start(f32[864,128]{1,0:T(8,128)S(1)} %get-tuple-element.503), channel_id=1, source_target_pairs={{0,16},{16,32},{32,48},{48,64},{64,80},{80,96},{96,112},{112,128},... | collective-permute-start | bytes 1327112 | tf_op jit(solution)/shard_map/while/body/eval_jaxpr/ppermute | solution.py:28
  356.1 21.1 %all-to-all-start = ((f32[16,64,128]{2,1,0:T(8,128)}), f32[16,64,128]{2,1,0:T(8,128)S(1)}, u32[]{:S(2)}, u32[]{:S(2)}) async-start(f32[16,64,128]{2,1,0:T(8,128)} %bitcast.61), calls=%async_computation | async-start | bytes 1048576 | tf_op jit(solution)/shard_map/while/body/eval_jaxpr/all_to_all | solution.py:82
  380.3 12.3 %collective-permute-start = (f32[864,128]{1,0:T(8,128)S(1)}, f32[864,128]{1,0:T(8,128)S(1)}, u32[]{:S(2)}, u32[]{:S(2)}) collective-permute-start(f32[864,128]{1,0:T(8,128)S(1)} %get-tuple-element.503), channel_id=1, source_target_pairs={{0,16},{16,32},{32,48},{48,64},{64,80},{80,96},{96,112},{112,128},... | collective-permute-start | bytes 1327112 | tf_op jit(solution)/shard_map/while/body/eval_jaxpr/ppermute | solution.py:28
  397.5 19.5 %all-to-all-start = ((f32[16,64,128]{2,1,0:T(8,128)}), f32[16,64,128]{2,1,0:T(8,128)S(1)}, u32[]{:S(2)}, u32[]{:S(2)}) async-start(f32[16,64,128]{2,1,0:T(8,128)} %bitcast.61), calls=%async_computation | async-start | bytes 1048576 | tf_op jit(solution)/shard_map/while/body/eval_jaxpr/all_to_all | solution.py:82
  420.1 12.1 %collective-permute-start = (f32[864,128]{1,0:T(8,128)S(1)}, f32[864,128]{1,0:T(8,128)S(1)}, u32[]{:S(2)}, u32[]{:S(2)}) collective-permute-start(f32[864,128]{1,0:T(8,128)S(1)} %get-tuple-element.503), channel_id=1, source_target_pairs={{0,16},{16,32},{32,48},{48,64},{64,80},{80,96},{96,112},{112,128},... | collective-permute-start | bytes 1327112 | tf_op jit(solution)/shard_map/while/body/eval_jaxpr/ppermute | solution.py:28
  437.1 21.3 %all-to-all-start = ((f32[16,64,128]{2,1,0:T(8,128)}), f32[16,64,128]{2,1,0:T(8,128)S(1)}, u32[]{:S(2)}, u32[]{:S(2)}) async-start(f32[16,64,128]{2,1,0:T(8,128)} %bitcast.61), calls=%async_computation | async-start | bytes 1048576 | tf_op jit(solution)/shard_map/while/body/eval_jaxpr/all_to_all | solution.py:82
  461.5 12.1 %collective-permute-start = (f32[864,128]{1,0:T(8,128)S(1)}, f32[864,128]{1,0:T(8,128)S(1)}, u32[]{:S(2)}, u32[]{:S(2)}) collective-permute-start(f32[864,128]{1,0:T(8,128)S(1)} %get-tuple-element.503), channel_id=1, source_target_pairs={{0,16},{16,32},{32,48},{48,64},{64,80},{80,96},{96,112},{112,128},... | collective-permute-start | bytes 1327112 | tf_op jit(solution)/shard_map/while/body/eval_jaxpr/ppermute | solution.py:28
  478.4 20.8 %all-to-all-start = ((f32[16,64,128]{2,1,0:T(8,128)}), f32[16,64,128]{2,1,0:T(8,128)S(1)}, u32[]{:S(2)}, u32[]{:S(2)}) async-start(f32[16,64,128]{2,1,0:T(8,128)} %bitcast.61), calls=%async_computation | async-start | bytes 1048576 | tf_op jit(solution)/shard_map/while/body/eval_jaxpr/all_to_all | solution.py:82
  502.3 12.1 %collective-permute-start = (f32[864,128]{1,0:T(8,128)S(1)}, f32[864,128]{1,0:T(8,128)S(1)}, u32[]{:S(2)}, u32[]{:S(2)}) collective-permute-start(f32[864,128]{1,0:T(8,128)S(1)} %get-tuple-element.503), channel_id=1, source_target_pairs={{0,16},{16,32},{32,48},{48,64},{64,80},{80,96},{96,112},{112,128},... | collective-permute-start | bytes 1327112 | tf_op jit(solution)/shard_map/while/body/eval_jaxpr/ppermute | solution.py:28
  519.2 20.1 %all-to-all-start = ((f32[16,64,128]{2,1,0:T(8,128)}), f32[16,64,128]{2,1,0:T(8,128)S(1)}, u32[]{:S(2)}, u32[]{:S(2)}) async-start(f32[16,64,128]{2,1,0:T(8,128)} %bitcast.61), calls=%async_computation | async-start | bytes 1048576 | tf_op jit(solution)/shard_map/while/body/eval_jaxpr/all_to_all | solution.py:82
  542.5 12.1 %collective-permute-start = (f32[864,128]{1,0:T(8,128)S(1)}, f32[864,128]{1,0:T(8,128)S(1)}, u32[]{:S(2)}, u32[]{:S(2)}) collective-permute-start(f32[864,128]{1,0:T(8,128)S(1)} %get-tuple-element.503), channel_id=1, source_target_pairs={{0,16},{16,32},{32,48},{48,64},{64,80},{80,96},{96,112},{112,128},... | collective-permute-start | bytes 1327112 | tf_op jit(solution)/shard_map/while/body/eval_jaxpr/ppermute | solution.py:28
  559.4 21.2 %all-to-all-start = ((f32[16,64,128]{2,1,0:T(8,128)}), f32[16,64,128]{2,1,0:T(8,128)S(1)}, u32[]{:S(2)}, u32[]{:S(2)}) async-start(f32[16,64,128]{2,1,0:T(8,128)} %bitcast.61), calls=%async_computation | async-start | bytes 1048576 | tf_op jit(solution)/shard_map/while/body/eval_jaxpr/all_to_all | solution.py:82
  583.8 12.2 %collective-permute-start = (f32[864,128]{1,0:T(8,128)S(1)}, f32[864,128]{1,0:T(8,128)S(1)}, u32[]{:S(2)}, u32[]{:S(2)}) collective-permute-start(f32[864,128]{1,0:T(8,128)S(1)} %get-tuple-element.503), channel_id=1, source_target_pairs={{0,16},{16,32},{32,48},{48,64},{64,80},{80,96},{96,112},{112,128},... | collective-permute-start | bytes 1327112 | tf_op jit(solution)/shard_map/while/body/eval_jaxpr/ppermute | solution.py:28
  600.9 19.7 %all-to-all-start = ((f32[16,64,128]{2,1,0:T(8,128)}), f32[16,64,128]{2,1,0:T(8,128)S(1)}, u32[]{:S(2)}, u32[]{:S(2)}) async-start(f32[16,64,128]{2,1,0:T(8,128)} %bitcast.61), calls=%async_computation | async-start | bytes 1048576 | tf_op jit(solution)/shard_map/while/body/eval_jaxpr/all_to_all | solution.py:82
  623.7 12.1 %collective-permute-start = (f32[864,128]{1,0:T(8,128)S(1)}, f32[864,128]{1,0:T(8,128)S(1)}, u32[]{:S(2)}, u32[]{:S(2)}) collective-permute-start(f32[864,128]{1,0:T(8,128)S(1)} %get-tuple-element.503), channel_id=1, source_target_pairs={{0,16},{16,32},{32,48},{48,64},{64,80},{80,96},{96,112},{112,128},... | collective-permute-start | bytes 1327112 | tf_op jit(solution)/shard_map/while/body/eval_jaxpr/ppermute | solution.py:28
  640.7 18.1 %all-to-all-start = ((f32[16,64,128]{2,1,0:T(8,128)}), f32[16,64,128]{2,1,0:T(8,128)S(1)}, u32[]{:S(2)}, u32[]{:S(2)}) async-start(f32[16,64,128]{2,1,0:T(8,128)} %bitcast.61), calls=%async_computation | async-start | bytes 1048576 | tf_op jit(solution)/shard_map/while/body/eval_jaxpr/all_to_all | solution.py:82
  661.8 0.9 copy-start
where the time goes:
time: 667 us; the launch traced here: 663 us
  waiting for transfers between devices  380 us (57%)
  local copies, waits for them, and re-layouts  124 us (19%)
  starting transfers between devices  70.8 us (11%)
  matrix products  59 us (9%)
  other arithmetic  26.7 us (4%)
    all_to_all x16, waiting for transfers between devices, handle(): lax.all_to_all(outgoing, 'vel', split_axis=0, concat_axis=0, tiled=True)  237 us
    ppermute x15, waiting for transfers between devices, shifted(): return lax.ppermute(value, axis, pairs)  140 us
    all_to_all x16, starting transfers between devices, handle(): lax.all_to_all(outgoing, 'vel', split_axis=0, concat_axis=0, tiled=True)  65.6 us
    gather x16, local copies, waits for them, and re-layouts, pair_terms(): outgoing = product[proj_pair[0, partner]]  64.4 us
    dot_general x16, matrix products, take_gain(): jnp.dot(one_hot, received, precision=lax.Precision.HIGHEST, preferred_ele...  49.5 us
  transfers between devices with their start and end apart: 33, of which 32 were waited for; matrix products, arithmetic and copies ran while one was open for 12% of the time, Pallas kernels for 0%

commit v1 on v0

v1 whole, which is shorter than its diff:
```python
import functools

import jax
import jax.numpy as jnp
from jax import lax
from jax.experimental import pallas as pl
from jax.experimental.pallas import tpu as pltpu
from jax.sharding import PartitionSpec as P

VSIDE = 24
MESH = pl.DeviceIdType.MESH
ROWS = 864
HALF = 432
KPAD = 512
F32 = jnp.float32
BF16 = jnp.bfloat16


def split(value):
    high = value.astype(BF16)
    return high, (value - high.astype(F32)).astype(BF16)


def kernel(
    dist, first, second, weight, picks, target, coef,
    out_t, out_c,
    edge_out, edge_in, packed, ring, sends_idx, idx, pairs_i, pairs_w, target_all, coef_all,
    wts, xs, ys, prod, prod_row, lossq, lossq_row, gain, loss, final,
    edge_s, edge_r, part_s, part_r, ring_s, ring_r, zidx_s, zidx_r, xidx_s, xidx_r, cidx_s, cidx_r,
    arg_s, arg_r, fin_s, fin_r,
):
    vel = lax.axis_index("vel")
    cell = lax.axis_index("cell")
    z = vel // 2
    x = vel % 2
    y = 1 - x
    core = cell % 2
    sibling = cell + 1 - 2 * core
    left = (cell + 15) % 16
    right = (cell + 1) % 16

    def at_z(steps, col=None):
        return {"vel": ((z + steps + 8) % 8) * 2 + (x if col is None else col)}

    partner = at_z(0, y)
    barrier = pltpu.get_barrier_semaphore()
    for steps in range(1, 8):
        pl.semaphore_signal(barrier, inc=1, device_id=at_z(steps), device_id_type=MESH)
    pl.semaphore_signal(barrier, inc=1, device_id=partner, device_id_type=MESH)
    for side in (left, right):
        pl.semaphore_signal(barrier, inc=1, device_id={"cell": side}, device_id_type=MESH)

    def send(src, dst, s_sem, r_sem, device):
        copy = pltpu.make_async_remote_copy(
            src_ref=src, dst_ref=dst, send_sem=s_sem, recv_sem=r_sem, device_id=device, device_id_type=MESH
        )
        copy.start()
        return copy

    lane8 = lax.broadcasted_iota(jnp.int32, (8, 128), 1)
    sub8 = lax.broadcasted_iota(jnp.int32, (8, 128), 0)
    pick = jnp.where(lane8 == 127 * sub8, 1.0, 0.0).astype(F32)
    edges = lax.dot_general(
        pick, dist[...], (((1,), (1,)), ((), ())), precision=lax.Precision.HIGHEST, preferred_element_type=F32
    )
    edge_out[0] = edges[1:2]
    edge_out[1] = edges[0:1]

    for b in range(8):
        take = picks[core, b]
        low = take & 127
        upper = take >= 128
        lane_first = lane8 < 64
        for kind, table in enumerate((first, second, weight)):
            rows = []
            for half in range(2):
                group = 2 * b + (half + x) % 2
                for part in range(2):
                    row = table[pl.ds(group * 2 + part, 1), :]
                    row = jnp.broadcast_to(row, (8, 128))
                    rows.append(jnp.take_along_axis(row, low, axis=1, mode="promise_in_bounds"))
            value = jnp.where(
                lane_first, jnp.where(upper, rows[1], rows[0]), jnp.where(upper, rows[3], rows[2])
            ).astype(F32)
            for owner in range(8):
                sends_idx[owner, pl.ds(kind * 8 + b, 1), :] = value[owner : owner + 1]

    pl.semaphore_wait(barrier, 10)

    edge_copies = [
        send(edge_out.at[0], edge_in.at[0], edge_s.at[0], edge_r.at[0], {"cell": right}),
        send(edge_out.at[1], edge_in.at[1], edge_s.at[1], edge_r.at[1], {"cell": left}),
    ]
    z_copies = [
        send(sends_idx.at[(z + k) % 8], idx.at[core, x, z], zidx_s.at[k], zidx_r.at[k], at_z(k)) for k in range(1, 8)
    ]
    idx[core, x, pl.ds(z, 1)] = sends_idx[pl.ds(z, 1)]
    pairs_i[x, 0] = first[...]
    pairs_i[x, 1] = second[...]
    pairs_w[x] = weight[...]
    arg_copies = [
        send(first, pairs_i.at[x, 0], arg_s.at[0], arg_r.at[0], partner),
        send(second, pairs_i.at[x, 1], arg_s.at[1], arg_r.at[1], partner),
        send(weight, pairs_w.at[x], arg_s.at[2], arg_r.at[2], partner),
        send(coef, coef_all.at[x], arg_s.at[3], arg_r.at[3], partner),
        send(target, target_all.at[x], arg_s.at[4], arg_r.at[4], partner),
    ]
    coef_all[x] = coef[...]
    target_all[x] = target[...]

    for copy in edge_copies:
        copy.wait_recv()
    node = vel * ROWS + lax.broadcasted_iota(jnp.int32, (ROWS, 128), 0)
    courant = (2 * (node // (VSIDE * VSIDE)) - VSIDE + 1).astype(F32) / (2.0 * VSIDE)
    lane = lax.broadcasted_iota(jnp.int32, (ROWS, 128), 1)
    here = dist[...]

    def column(row):
        return jnp.broadcast_to(row, (8, ROWS)).T[:, 0:1]

    before = jnp.where(lane == 0, column(edge_in[0]), pltpu.roll(here, 1, axis=1))
    after = jnp.where(lane == 127, column(edge_in[1]), pltpu.roll(here, 127, axis=1))
    moved = here - jnp.maximum(courant, 0.0) * (here - before) - jnp.minimum(courant, 0.0) * (after - here)
    out_t[...] = moved
    top, low = moved[:HALF], moved[HALF:]
    lane_low = lax.broadcasted_iota(jnp.int32, (HALF, 128), 1) < 64
    packed[0] = jnp.where(lane_low, top, pltpu.roll(low, 64, axis=1))
    packed[1] = jnp.where(lane_low, pltpu.roll(top, 64, axis=1), low)
    part_copy = send(packed.at[y], ring.at[0, x], part_s, part_r, partner)
    ring[0, pl.ds(x, 1)] = packed[pl.ds(x, 1)]

    def ring_copy(way, step, src_m, dst_m, group):
        return pltpu.make_async_remote_copy(
            src_ref=ring.at[src_m, group],
            dst_ref=ring.at[dst_m, group],
            send_sem=ring_s.at[way, step],
            recv_sem=ring_r.at[way, step],
            device_id=at_z(1 - 2 * way),
            device_id_type=MESH,
        )

    ring_copy(0, 1, 0, 1, x).start()
    ring_copy(1, 1, 0, 2, x).start()

    gain[...] = jnp.zeros_like(gain)
    loss[...] = jnp.zeros_like(loss)
    wts[...] = jnp.zeros_like(wts)

    part_copy.wait_send()
    part_copy.wait_recv()
    ring_copy(0, 2, 0, 1, y).start()
    ring_copy(1, 2, 0, 2, y).start()

    for copy in z_copies:
        copy.wait_recv()
    x_copy = send(idx.at[core, x], idx.at[core, x], xidx_s, xidx_r, partner)
    for copy in arg_copies:
        copy.wait_recv()
    x_copy.wait_recv()
    c_copy = send(idx.at[core], idx.at[core], cidx_s, cidx_r, {"cell": sibling})
    c_copy.wait_recv()

    def place(m):
        return (z + (m % 2) * (8 - (m + 1) // 2) + (1 - m % 2) * (m // 2)) % 8

    slot_iota = lax.broadcasted_iota(jnp.int32, (KPAD, 18 * 128), 0).astype(F32)
    row_low = lax.broadcasted_iota(jnp.int32, (1, 128), 1) < 64

    def gather_group(m, group, sequence):
        zz = place(m)
        actual = 2 * zz + group
        turned = ring[m, group].T
        high, rest = split(turned)
        wts[0:128, 0:HALF] = high
        wts[128:256, 0:HALF] = rest

        def gather(e, carry):
            rows = [idx[e, group, zz, b : b + 1, :] for b in range(8)]
            for a in range(8):
                even = idx[e, 0, a, pl.ds(8 + zz, 1), :]
                odd = idx[e, 1, a, pl.ds(8 + zz, 1), :]
                rows.append(jnp.where(row_low == (group == 0), even, odd))
            rows.append(pairs_i[e, 1, pl.ds(actual * 2, 1), :].astype(F32))
            rows.append(pairs_i[e, 1, pl.ds(actual * 2 + 1, 1), :].astype(F32))
            nodes = jnp.concatenate(rows, axis=1)
            upper = nodes >= float(HALF)
            local = jnp.where(upper, nodes - float(HALF), nodes)
            one_hot = jnp.where(slot_iota == local, 1.0, 0.0).astype(BF16)
            found = jnp.dot(wts[...], one_hot, preferred_element_type=F32)
            found = found[0:128] + found[128:256]
            found = jnp.where(upper, found[64:128], found[0:64])
            for b in range(8):
                scale = idx[e, group, zz, 16 + b : 17 + b, :] * coef_all[e, actual, b : b + 1, :]
                xs[m, group, e, b] = found[:, b * 128 : b * 128 + 128] * scale
                ys[m, group, e, b] = found[:, 1024 + b * 128 : 1024 + b * 128 + 128]
            for part in range(2):
                term = found[:, 2048 + part * 128 : 2048 + part * 128 + 128]
                term = term * pairs_w[e, pl.ds(actual * 2 + part, 1), :]
                goal = pairs_i[e, 0, pl.ds(actual * 2 + part, 1), :]
                put(lossq, lossq_row, e, (sequence % 4) * 2 + part, term, goal)
            return carry

        lax.fori_loop(0, 2, gather, 0)

    def put(queue, queue_row, e, tile, term, goal):
        upper = goal >= HALF
        high, rest = split(jnp.concatenate([jnp.where(upper, 0.0, term), jnp.where(upper, term, 0.0)], axis=0))
        queue[e, tile, 0:128] = high
        queue[e, tile, 128:256] = rest
        queue_row[e, tile] = jnp.where(upper, goal - HALF, goal)

    def add_up(total, queue, queue_row, e, tiles):
        goal = jnp.concatenate([queue_row[e, i] for i in range(tiles)], axis=1)
        node_iota = lax.broadcasted_iota(jnp.int32, (HALF, tiles * 128), 0)
        one_hot = jnp.where(node_iota == goal, 1.0, 0.0).astype(BF16)
        terms = jnp.concatenate([queue[e, i] for i in range(tiles)], axis=1)
        total[e] += lax.dot_general(one_hot, terms, (((1,), (1,)), ((), ())), preferred_element_type=F32)

    tile_low = lax.broadcasted_iota(jnp.int32, (64, 128), 1) < 64

    def chunk(c, carry):
        def one_owner(e, inner):
            def block(i, deep):
                n = c * 8 + i
                m = sum([(n + 64 - k * k) // 64 for k in range(1, 8)])
                d = n - m * m
                later = (d + 7 - m) // 8
                ma = (1 - later) * m + later * (d - m - 1)
                mb = (1 - later) * d + later * m
                za, zb = place(ma), place(mb)
                even, odd = xs[ma, 0, e, zb], xs[ma, 1, e, zb]
                put(prod, prod_row, e, 2 * i, jnp.where(tile_low, even, odd) * ys[mb, 0, e, za],
                    target_all[e, za, zb, 0:1, :])
                put(prod, prod_row, e, 2 * i + 1, jnp.where(tile_low, odd, even) * ys[mb, 1, e, za],
                    target_all[e, za, zb, 1:2, :])
                return deep

            lax.fori_loop(0, 8, block, 0)
            add_up(gain, prod, prod_row, e, 16)
            return inner

        lax.fori_loop(0, 2, one_owner, 0)
        return carry

    def step(t, carry):
        k = (t + 1) // 2
        group = (x + t + 1) % 2

        @pl.when(t >= 1)
        def _():
            last = t // 7
            m0 = 2 * k - 1
            m1 = 2 * k - last
            ring_copy(0, t, m0, m0, (1 - last) * group).wait_recv()
            ring_copy(1, t, m1, m1, (1 - last) * group + last).wait_recv()

        @pl.when((t >= 1) & (t <= 4))
        def _():
            ring_copy(0, t + 2, 2 * k - 1, 2 * k + 1, group).start()
            ring_copy(1, t + 2, 2 * k, 2 * k + 2, group).start()

        @pl.when((t >= 5) & (t <= 6))
        def _():
            ring_copy(group, 7, 5 + group, 7, group).start()

        def one(i, inner):
            ends = (t // 7) + (7 - t) // 7
            m = (1 - ends) * (2 * k - 1 + i) + (t // 7) * 7
            g = (1 - ends) * group + ends * i
            gather_group(m, g, 2 * t + i)
            return inner

        lax.fori_loop(0, 2, one, 0)

        @pl.when(t % 2 == 1)
        def _():
            def lossy(e, inner):
                add_up(loss, lossq, lossq_row, e, 8)
                return inner

            lax.fori_loop(0, 2, lossy, 0)

        def ready(t):
            return (t // 2) * (t // 2 + 1) // 2 + 2 * (t // 7)

        before_t = jnp.where(t > 0, ready(jnp.maximum(t - 1, 0)), 0)
        lax.fori_loop(before_t, ready(t), chunk, 0)
        return carry

    lax.fori_loop(0, 8, step, 0)

    def finish(e):
        g = gain[e]
        s = loss[e]
        return g[:, 0:128] + g[:, 128:256] - ring[0, e] * (s[:, 0:128] + s[:, 128:256])

    packed[0] = finish(y)
    fin_copy = send(packed.at[0], final.at[x], fin_s, fin_r, partner)
    final[pl.ds(x, 1)] = finish(x)[None]
    fin_copy.wait_recv()
    lo, hi = final[0], final[1]
    out_c[0:HALF, :] = jnp.where(lane_low, lo, pltpu.roll(hi, 64, axis=1))
    out_c[HALF:ROWS, :] = jnp.where(lane_low, pltpu.roll(lo, 64, axis=1), hi)

    for copy in edge_copies + z_copies + arg_copies + [x_copy, c_copy, fin_copy]:
        copy.wait_send()

    def drain(t, carry):
        m0 = 0
        ring_copy(0, t, m0, m0, 0).wait_send()
        ring_copy(1, t, m0, m0, 0).wait_send()
        return carry

    lax.fori_loop(1, 8, drain, 0)


def on_device(distribution, pair_first, pair_second, pair_weight, proj_pair, proj_target, proj_coef, slot_counts):
    x = lax.axis_index("vel") % 2
    picks = proj_pair.reshape(8, 2, 8, 2, 64)
    picks = jnp.where(x == 1, picks[:, ::-1], picks)
    picks = picks.transpose(3, 0, 2, 1, 4).reshape(2, 8, 8, 128)
    live = jnp.arange(64, dtype=jnp.int32) < slot_counts[:, :, :, None]
    coef = jnp.where(live, proj_coef, 0.0).reshape(8, 2, 8, 2, 64)
    coef = jnp.stack([coef[:, 0], coef[:, 1, :, ::-1]], axis=1).reshape(16, 8, 128)
    goal = proj_target.reshape(8, 2, 8, 2, 64)
    goal = jnp.stack([goal[:, :, :, 0], goal[:, ::-1, :, 1]], axis=1)
    goal = goal.transpose(0, 3, 1, 2, 4).reshape(8, 8, 2, 128)

    vmem = pl.BlockSpec(memory_space=pltpu.VMEM)
    dma = pltpu.SemaphoreType.DMA
    return pl.pallas_call(
        kernel,
        out_shape=(jax.ShapeDtypeStruct((ROWS, 128), F32), jax.ShapeDtypeStruct((ROWS, 128), F32)),
        in_specs=[vmem] * 7,
        out_specs=(vmem, vmem),
        scratch_shapes=[
            pltpu.VMEM((2, 1, ROWS), F32),
            pltpu.VMEM((2, 1, ROWS), F32),
            pltpu.VMEM((2, HALF, 128), F32),
            pltpu.VMEM((8, 2, HALF, 128), F32),
            pltpu.VMEM((8, 24, 128), F32),
            pltpu.VMEM((2, 2, 8, 24, 128), F32),
            pltpu.VMEM((2, 2, 32, 128), jnp.int32),
            pltpu.VMEM((2, 32, 128), F32),
            pltpu.VMEM((2, 8, 8, 2, 128), jnp.int32),
            pltpu.VMEM((2, 16, 8, 128), F32),
            pltpu.VMEM((256, KPAD), BF16),
            pltpu.VMEM((8, 2, 2, 8, 64, 128), F32),
            pltpu.VMEM((8, 2, 2, 8, 64, 128), F32),
            pltpu.VMEM((2, 16, 256, 128), BF16),
            pltpu.VMEM((2, 16, 1, 128), jnp.int32),
            pltpu.VMEM((2, 8, 256, 128), BF16),
            pltpu.VMEM((2, 8, 1, 128), jnp.int32),
            pltpu.VMEM((2, HALF, 256), F32),
            pltpu.VMEM((2, HALF, 256), F32),
            pltpu.VMEM((2, HALF, 128), F32),
            dma((2,)), dma((2,)), dma, dma, dma((2, 8)), dma((2, 8)), dma((8,)), dma((8,)), dma, dma, dma, dma,
            dma((5,)), dma((5,)), dma, dma,
        ],
        compiler_params=pltpu.CompilerParams(
            collective_id=0, has_side_effects=True, vmem_limit_bytes=60 << 20
        ),
    )(
        distribution,
        pair_first.reshape(32, 128),
        pair_second.reshape(32, 128),
        pair_weight.reshape(32, 128),
        picks,
        goal,
        coef,
    )


def solution(mesh):
    in_specs = (
        P("vel", "cell"),
        P("vel", None, None),
        P("vel", None, None),
        P("vel", None, None),
        P("vel", None, None, None),
        P(None, None, "vel", None),
        P(None, None, "vel", None),
        P(None, None, "vel"),
    )
    out_specs = (P("vel", "cell"), P("vel", "cell"))
    return jax.shard_map(
        on_device, mesh=mesh, in_specs=in_specs, out_specs=out_specs, check_vma=False
    )
```

time: 667 us -> 105 us (0.16)
  waiting for transfers between devices: 380 us -> 0 us
  local copies, waits for them, and re-layouts: 124 us -> 10 us
  Pallas kernels: 0 us -> 92 us
  starting transfers between devices: 70.8 us -> 0 us
  matrix products: 59 us -> 0 us
  other arithmetic: 26.7 us -> 0.55 us
    all_to_all x16 -> x0, waiting for transfers between devices: 237 us -> none  [handle(): lax.all_to_all(outgoing, 'vel', split_axis=0, concat_axis=0, tiled=True)]
    ppermute x17 -> x0, waiting for transfers between devices: 143 us -> none  [the longest x15 140 us: shifted(): return lax.ppermute(value, axis, pairs)]
    gather x80 -> x0, local copies, waits for them, and re-layouts: 108 us -> none  [the longest x16 64.4 us: pair_terms(): outgoing = product[proj_pair[0, partner]]]
    pallas_call x0 -> x1, Pallas kernels: none -> 92 us  [on_device(): pl.pallas_call(kernel, out_shape=(jax.ShapeDtypeStruct((ROWS, 128), F32),...]
    all_to_all x16 -> x0, starting transfers between devices: 65.6 us -> none  [handle(): lax.all_to_all(outgoing, 'vel', split_axis=0, concat_axis=0, tiled=True)]
    dot_general x32 -> x0, matrix products: 59 us -> none  [the longest x16 49.5 us: take_gain(): jnp.dot(one_hot, received, precision=lax.Precision.HIGHEST, preferred_ele...]
    select_n x32 -> x1, other arithmetic: 22.9 us -> 0.33 us  [on_device(): coef = jnp.where(live, proj_coef, 0.0).reshape(8, 2, 8, 2, 64)]
    dynamic_slice x16 -> x0, local copies, waits for them, and re-layouts: 11.2 us -> none  [pair_terms(): pair_weight[0, partner][:, None] * transported[first_rows] * second_values]
  transfers between devices with their start and end apart: 33 -> 0, of which waited for: 32 -> 0; matrix products, arithmetic and copies ran while one was open for 12% -> 0% of each run, Pallas kernels for 0% -> 0%
where the time goes in v1:
time: 105 us; the launch traced here: 103 us
  Pallas kernels  92 us (88%)
  local copies, waits for them, and re-layouts  10 us (10%)
    pallas_call x1, Pallas kernels, on_device(): pl.pallas_call(kernel, out_shape=(jax.ShapeDtypeStruct((ROWS, 128), F32),...  92 us
    unnamed x14, local copies, waits for them, and re-layouts  2.99 us

profile of v1, /device:TPU:16, one launch (start us, length us, event | category | flops | bytes accessed | tf_op | source)
XLA Modules:
  0.0 103.3 jit_solution(759868758298988432)
XLA Ops:
  0.6 0.0 copy-start
  0.7 1.4 %reshape.42.first = s32[32,128]{1,0:T(8,128)} reshape(s32[1,16,256]{2,1,0:T(8,128)} %param.9) | data formatting | bytes 32768 | tf_op jit(solution)/shard_map/reshape | solution.py:365
  2.0 1.3 %reshape.43.second = s32[32,128]{1,0:T(8,128)} reshape(s32[1,16,256]{2,1,0:T(8,128)} %param.10) | data formatting | bytes 32768 | tf_op jit(solution)/shard_map/reshape | solution.py:366
  3.3 1.3 %reshape.44.weight = f32[32,128]{1,0:T(8,128)} reshape(f32[1,16,256]{2,1,0:T(8,128)} %param.11) | data formatting | bytes 32768 | tf_op jit(solution)/shard_map/reshape | solution.py:367
  4.7 0.0 copy-done
  4.7 0.1 copy.10
  4.7 0.3 rev.9
  5.0 0.1 select_bitcast_fusion
  5.1 0.0 copy-start.2
  5.1 0.0 copy-start.4
  5.1 0.8 reshape.46.picks
  5.9 0.1 copy-done.2
  6.0 0.0 copy-done.4
  6.0 0.3 compare_select_fusion
  6.4 0.2 rev.11
  6.5 0.1 pad_maximum_fusion
  6.6 0.0 copy-start.3
  6.6 0.7 reshape.50.coef
  7.4 0.2 copy-done.3
  7.5 0.1 fusion.1
  7.7 0.2 rev.10
  7.9 0.1 add_bitcast_fusion
  7.9 0.8 reshape.48.target
  8.7 92.0 %shard_map.95 = (f32[864,128]{1,0:T(8,128)}, f32[864,128]{1,0:T(8,128)}) custom-call(f32[864,128]{1,0:T(8,128)} %dist.1, s32[32,128]{1,0:T(8,128)} %reshape.42.first, s32[32,128]{1,0:T(8,128)} %reshape.43.second, f32[32,128]{1,0:T(8,128)} %reshape.44.weight, s32[2,8,8,128]{3,2,1,0:T(8,128)} %reshape.46.picks, s32[8,8,2,128]{3,2,1,0:T(2,128)} %reshape.48.target, ...), custom_call_target="tpu_custom_call" | custom-call | tf_op jit(solution)/shard_map/pallas_call | solution.py:331
  100.7 0.0 copy-start.1
  100.7 1.9 %copy.21 = f32[864,128]{1,0:T(8,128)} copy(f32[864,128]{1,0:T(8,128)} %get-tuple-element.8) | data formatting | bytes 884736
  102.6 0.0 copy-done.1
  102.6 0.8 copy.22
  (3 shorter events, 0.1 us)
Async XLA Ops:
  0.6 4.0 %copy-start = (s32[1,16,16,64]{3,2,1,0:T(8,128)S(1)}, s32[1,16,16,64]{3,2,1,0:T(8,128)}, u32[]{:S(2)}) copy-start(s32[1,16,16,64]{3,2,1,0:T(8,128)} %param.12) | copy-start | bytes 196612
  5.1 0.9 copy-start.2
  5.1 0.9 copy-start.4
  6.6 0.9 copy-start.3
  100.7 1.9 %copy-start.1 = (f32[864,128]{1,0:T(8,128)S(1)}, f32[864,128]{1,0:T(8,128)}, u32[]{:S(2)}) copy-start(f32[864,128]{1,0:T(8,128)} %get-tuple-element.9) | copy-start | bytes 1327108

commit v2 on v1

v2 whole, which is shorter than its diff:
```python
import functools

import jax
import jax.numpy as jnp
from jax import lax
from jax.experimental import pallas as pl
from jax.experimental.pallas import tpu as pltpu
from jax.sharding import PartitionSpec as P

VSIDE = 24
MESH = pl.DeviceIdType.MESH
ROWS = 864
HALF = 432
KPAD = 512
F32 = jnp.float32
BF16 = jnp.bfloat16


def split(value):
    high = value.astype(BF16)
    return high, (value - high.astype(F32)).astype(BF16)


def kernel(
    dist, first, second, weight, picks, target, coef, counts,
    out_t, out_c,
    edge_out, edge_in, packed, ring, sends_idx, idx, pairs, args, wts, xs, ys, lossq, lossq_row, gain, loss, final,
    edge_s, edge_r, part_s, part_r, ring_s, ring_r, zidx_s, zidx_r, xs_s, xs_r, cs_s, cs_r, fin_s, fin_r,
):
    vel = lax.axis_index("vel")
    cell = lax.axis_index("cell")
    z = vel // 2
    x = vel % 2
    y = 1 - x
    core = cell % 2
    left = (cell + 15) % 16
    right = (cell + 1) % 16

    def at_z(steps, col=None):
        return {"vel": ((z + steps + 8) % 8) * 2 + (x if col is None else col)}

    partner = at_z(0, y)
    sibling = {"cell": cell + 1 - 2 * core}
    barrier = pltpu.get_barrier_semaphore()
    for steps in range(1, 8):
        pl.semaphore_signal(barrier, inc=1, device_id=at_z(steps), device_id_type=MESH)
    pl.semaphore_signal(barrier, inc=1, device_id=partner, device_id_type=MESH)
    for side in (left, right):
        pl.semaphore_signal(barrier, inc=1, device_id={"cell": side}, device_id_type=MESH)

    def send(src, dst, s_sem, r_sem, device):
        copy = pltpu.make_async_remote_copy(
            src_ref=src, dst_ref=dst, send_sem=s_sem, recv_sem=r_sem, device_id=device, device_id_type=MESH
        )
        copy.start()
        return copy

    lane8 = lax.broadcasted_iota(jnp.int32, (8, 128), 1)
    sub8 = lax.broadcasted_iota(jnp.int32, (8, 128), 0)
    pick = jnp.where(lane8 == 127 * sub8, 1.0, 0.0).astype(F32)
    edges = lax.dot_general(
        pick, dist[...], (((1,), (1,)), ((), ())), precision=lax.Precision.HIGHEST, preferred_element_type=F32
    )
    edge_out[0] = edges[1:2]
    edge_out[1] = edges[0:1]

    for half in range(2):
        rows = slice(half * 8, half * 8 + 8)
        pairs[half, x, 0] = first[0, rows, :].astype(F32)
        pairs[half, x, 1] = second[0, rows, :].astype(F32)
        pairs[half, x, 2] = weight[0, rows, :]

    pl.semaphore_wait(barrier, 10)

    edge_copies = [
        send(edge_out.at[0], edge_in.at[0], edge_s.at[0], edge_r.at[0], {"cell": right}),
        send(edge_out.at[1], edge_in.at[1], edge_s.at[1], edge_r.at[1], {"cell": left}),
    ]
    pairs_copy = send(pairs.at[core, x], pairs.at[core, x], xs_s.at[0], xs_r.at[0], partner)

    for b in range(8):
        groups = [2 * b + (half + x) % 2 for half in range(2)]
        take = jnp.concatenate([picks[0, group, pl.ds(core, 8, stride=2), :] for group in groups], axis=1)
        low = take & 127
        upper = take >= 128
        lane_first = lane8 < 64
        for kind, table in enumerate((first, second, weight)):
            rows = []
            for group in groups:
                row = table[0, pl.ds(group, 1), :]
                for part in range(2):
                    piece = jnp.broadcast_to(row[:, part * 128 : part * 128 + 128], (8, 128))
                    rows.append(jnp.take_along_axis(piece, low, axis=1, mode="promise_in_bounds"))
            value = jnp.where(
                lane_first, jnp.where(upper, rows[1], rows[0]), jnp.where(upper, rows[3], rows[2])
            ).astype(F32)
            for owner in range(8):
                sends_idx[owner, pl.ds(kind * 8 + b, 1), :] = value[owner : owner + 1]
    z_copies = [
        send(sends_idx.at[(z + k) % 8], idx.at[core, x, z], zidx_s.at[k], zidx_r.at[k], at_z(k)) for k in range(1, 8)
    ]
    idx[core, x, pl.ds(z, 1)] = sends_idx[pl.ds(z, 1)]

    for copy in edge_copies:
        copy.wait_recv()
    node = vel * ROWS + lax.broadcasted_iota(jnp.int32, (ROWS, 128), 0)
    courant = (2 * (node // (VSIDE * VSIDE)) - VSIDE + 1).astype(F32) / (2.0 * VSIDE)
    lane = lax.broadcasted_iota(jnp.int32, (ROWS, 128), 1)
    here = dist[...]

    def column(row):
        return jnp.broadcast_to(row, (8, ROWS)).T[:, 0:1]

    before = jnp.where(lane == 0, column(edge_in[0]), pltpu.roll(here, 1, axis=1))
    after = jnp.where(lane == 127, column(edge_in[1]), pltpu.roll(here, 127, axis=1))
    moved = here - jnp.maximum(courant, 0.0) * (here - before) - jnp.minimum(courant, 0.0) * (after - here)
    out_t[...] = moved
    top, low = moved[:HALF], moved[HALF:]
    lane_low = lax.broadcasted_iota(jnp.int32, (HALF, 128), 1) < 64
    packed[0] = jnp.where(lane_low, top, pltpu.roll(low, 64, axis=1))
    packed[1] = jnp.where(lane_low, pltpu.roll(top, 64, axis=1), low)
    ring[0, pl.ds(x, 1)] = packed[pl.ds(x, 1)]

    def ring_copy(way, step, src_m, dst_m, group):
        return pltpu.make_async_remote_copy(
            src_ref=ring.at[src_m, group],
            dst_ref=ring.at[dst_m, group],
            send_sem=ring_s.at[way, step],
            recv_sem=ring_r.at[way, step],
            device_id=at_z(1 - 2 * way),
            device_id_type=MESH,
        )

    ring_copy(0, 1, 0, 1, x).start()
    ring_copy(1, 1, 0, 2, x).start()
    part_copy = send(packed.at[y], ring.at[0, x], part_s, part_r, partner)

    slot = lax.broadcasted_iota(jnp.int32, (8, 64), 1)
    for s in range(16):
        rows = []
        for half in range(2):
            every = pl.ds((half + s) % 2, 8, stride=2)
            rows.append(jnp.where(slot < counts[s, every, :], coef[s, every, 0, :], 0.0))
        args[0, x, s * 8 : s * 8 + 8] = jnp.concatenate(rows, axis=1)
    for a in range(8):
        for tile in range(2):
            every = pl.ds(tile, 8, stride=2)
            rows = [target[2 * a + (half + tile) % 2, every, 0, :] for half in range(2)]
            start = a * 16 + tile * 8
            args[1, x, start : start + 8] = jnp.concatenate(rows, axis=1).astype(F32)
    args_copy = send(args.at[core, x], args.at[core, x], xs_s.at[1], xs_r.at[1], partner)

    for copy in z_copies:
        copy.wait_recv()
    idx_copy = send(idx.at[core, x], idx.at[core, x], xs_s.at[2], xs_r.at[2], partner)

    gain[...] = jnp.zeros_like(gain)
    loss[...] = jnp.zeros_like(loss)
    wts[...] = jnp.zeros_like(wts)

    part_copy.wait_recv()
    ring_copy(0, 2, 0, 1, y).start()
    ring_copy(1, 2, 0, 2, y).start()

    pairs_copy.wait_recv()
    pairs_on = send(pairs.at[core, y], pairs.at[core, y], cs_s.at[0], cs_r.at[0], sibling)
    args_copy.wait_recv()
    args_on = send(args.at[core, y], args.at[core, y], cs_s.at[1], cs_r.at[1], sibling)
    idx_copy.wait_recv()
    idx_on = send(idx.at[core], idx.at[core], cs_s.at[2], cs_r.at[2], sibling)
    pairs_on.wait_recv()
    args_on.wait_recv()
    idx_on.wait_recv()

    def place(m):
        return (z + (m % 2) * (8 - (m + 1) // 2) + (1 - m % 2) * (m // 2)) % 8

    row_low = lax.broadcasted_iota(jnp.int32, (1, 128), 1) < 64

    def split_terms(term, upper):
        high, rest = split(jnp.concatenate([jnp.where(upper, 0.0, term), jnp.where(upper, term, 0.0)], axis=0))
        return jnp.concatenate([high, rest], axis=0)

    def gather_group(i, m, group, sequence, e):
        zz = place(m)
        actual = 2 * zz + group
        rows = [idx[e, group, zz, b : b + 1, :] for b in range(8)]
        for a in range(8):
            even = idx[e, 0, a, pl.ds(8 + zz, 1), :]
            odd = idx[e, 1, a, pl.ds(8 + zz, 1), :]
            rows.append(jnp.where(row_low == (group == 0), even, odd))
        pair_half, pair_row = zz // 4, pl.ds(actual % 8, 1)
        rows.append(pairs[pair_half, e, 1, pair_row, :])
        nodes = jnp.concatenate(rows, axis=1)
        upper = nodes >= float(HALF)
        local = jnp.where(upper, nodes - float(HALF), nodes)
        slot_iota = lax.broadcasted_iota(jnp.int32, (KPAD, 18 * 128), 0).astype(F32)
        one_hot = jnp.where(slot_iota == local, 1.0, 0.0).astype(BF16)
        found = jnp.dot(wts[i], one_hot, preferred_element_type=F32)
        found = found[0:128] + found[128:256]
        found = jnp.where(upper, found[64:128], found[0:64])
        for b in range(8):
            scale = idx[e, group, zz, 16 + b : 17 + b, :] * args[0, e, pl.ds(actual * 8 + b, 1), :]
            xs[m, group, e, b] = found[:, b * 128 : b * 128 + 128] * scale
            ys[m, group, e, b] = found[:, 1024 + b * 128 : 1024 + b * 128 + 128]
        share = pairs[pair_half, e, 2, pair_row, :]
        goal = pairs[pair_half, e, 0, pair_row, :]
        upper = goal >= float(HALF)
        terms = split_terms(found[:, 2048:2304] * share, upper)
        goal = jnp.where(upper, goal - float(HALF), goal)
        for part in range(2):
            tile = (sequence % 4) * 2 + part
            lossq[e, tile] = terms[:, part * 128 : part * 128 + 128]
            lossq_row[e, tile] = goal[:, part * 128 : part * 128 + 128]

    def scatter(goals, terms):
        goal = jnp.concatenate(goals, axis=1)
        node_iota = lax.broadcasted_iota(jnp.int32, (HALF, len(goals) * 128), 0).astype(F32)
        one_hot = jnp.where(node_iota == goal, 1.0, 0.0).astype(BF16)
        return lax.dot_general(
            one_hot, jnp.concatenate(terms, axis=1), (((1,), (1,)), ((), ())), preferred_element_type=F32
        )

    tile_low = lax.broadcasted_iota(jnp.int32, (64, 128), 1) < 64

    def chunk(c, e):
        goals, terms = [], []
        for i in range(8):
            n = c * 8 + i
            m = sum([(n + 64 - k * k) // 64 for k in range(1, 8)])
            d = n - m * m
            later = (d + 7 - m) // 8
            ma = (1 - later) * m + later * (d - m - 1)
            mb = (1 - later) * d + later * m
            za, zb = place(ma), place(mb)
            even, odd = xs[ma, 0, e, zb], xs[ma, 1, e, zb]
            for tile in range(2):
                mine = jnp.where(tile_low, even, odd) if tile == 0 else jnp.where(tile_low, odd, even)
                goal = args[1, e, pl.ds(za * 16 + tile * 8 + zb, 1), :]
                upper = goal >= float(HALF)
                terms.append(split_terms(mine * ys[mb, tile, e, za], upper))
                goals.append(jnp.where(upper, goal - float(HALF), goal))
        gain[e] += scatter(goals, terms)
        return e

    def finish(e):
        g = gain[e]
        s = loss[e]
        return g[:, 0:128] + g[:, 128:256] - ring[0, e] * (s[:, 0:128] + s[:, 128:256])

    def final_copy():
        return pltpu.make_async_remote_copy(
            src_ref=packed.at[0], dst_ref=final.at[x], send_sem=fin_s, recv_sem=fin_r, device_id=partner,
            device_id_type=MESH,
        )

    part_copy.wait_send()

    def step(t, carry):
        k = (t + 1) // 2
        group = (x + t + 1) % 2
        last = t // 7

        @pl.when(t >= 1)
        def _():
            m0 = 2 * k - 1
            m1 = 2 * k - last
            ring_copy(0, t, m0, m0, (1 - last) * group).wait_recv()
            ring_copy(1, t, m1, m1, (1 - last) * group + last).wait_recv()

        @pl.when((t >= 1) & (t <= 4))
        def _():
            ring_copy(0, t + 2, 2 * k - 1, 2 * k + 1, group).start()
            ring_copy(1, t + 2, 2 * k, 2 * k + 2, group).start()

        @pl.when((t >= 5) & (t <= 6))
        def _():
            ring_copy(group, 7, 5 + group, 7, group).start()

        ends = last + (7 - t) // 7
        arrived = []
        for i in range(2):
            m = (1 - ends) * (2 * k - 1 + i) + last * 7
            g = (1 - ends) * group + ends * i
            arrived.append((m, g))
            high, rest = split(ring[m, g].T)
            wts[i, 0:128, 0:HALF] = high
            wts[i, 128:256, 0:HALF] = rest

        def ready(t):
            return (t // 2) * (t // 2 + 1) // 2 + 2 * (t // 7)

        from_chunk = ready(t - 1 + (7 - t) // 7)

        def one_owner(turn, inner):
            e = (y + turn) % 2
            for i in range(2):
                gather_group(i, *arrived[i], 2 * t + i, e)

            @pl.when(t % 2 == 1)
            def _():
                loss[e] += scatter([lossq_row[e, i] for i in range(8)], [lossq[e, i] for i in range(8)])

            lax.fori_loop(from_chunk, ready(t), chunk, e)

            @pl.when((t == 7) & (turn == 0))
            def _():
                packed[0] = finish(y)
                final_copy().start()

            return inner

        lax.fori_loop(0, 2, one_owner, 0)
        return carry

    lax.fori_loop(0, 8, step, 0)

    final[pl.ds(x, 1)] = finish(x)[None]
    final_copy().wait_recv()
    lo, hi = final[0], final[1]
    out_c[0:HALF, :] = jnp.where(lane_low, lo, pltpu.roll(hi, 64, axis=1))
    out_c[HALF:ROWS, :] = jnp.where(lane_low, pltpu.roll(lo, 64, axis=1), hi)

    final_copy().wait_send()
    for copy in edge_copies + z_copies + [pairs_copy, args_copy, idx_copy, pairs_on, args_on, idx_on]:
        copy.wait_send()

    def drain(t, carry):
        ring_copy(0, t, 0, 0, 0).wait_send()
        ring_copy(1, t, 0, 0, 0).wait_send()
        return carry

    lax.fori_loop(1, 8, drain, 0)


def on_device(distribution, pair_first, pair_second, pair_weight, proj_pair, proj_target, proj_coef, slot_counts):
    vmem = pl.BlockSpec(memory_space=pltpu.VMEM)
    dma = pltpu.SemaphoreType.DMA
    return pl.pallas_call(
        kernel,
        out_shape=(jax.ShapeDtypeStruct((ROWS, 128), F32), jax.ShapeDtypeStruct((ROWS, 128), F32)),
        in_specs=[vmem] * 8,
        out_specs=(vmem, vmem),
        scratch_shapes=[
            pltpu.VMEM((2, 1, ROWS), F32),
            pltpu.VMEM((2, 1, ROWS), F32),
            pltpu.VMEM((2, HALF, 128), F32),
            pltpu.VMEM((8, 2, HALF, 128), F32),
            pltpu.VMEM((8, 24, 128), F32),
            pltpu.VMEM((2, 2, 8, 24, 128), F32),
            pltpu.VMEM((2, 2, 3, 8, 256), F32),
            pltpu.VMEM((2, 2, 128, 128), F32),
            pltpu.VMEM((2, 256, KPAD), BF16),
            pltpu.VMEM((8, 2, 2, 8, 64, 128), F32),
            pltpu.VMEM((8, 2, 2, 8, 64, 128), F32),
            pltpu.VMEM((2, 8, 256, 128), BF16),
            pltpu.VMEM((2, 8, 1, 128), F32),
            pltpu.VMEM((2, HALF, 256), F32),
            pltpu.VMEM((2, HALF, 256), F32),
            pltpu.VMEM((2, HALF, 128), F32),
            dma((2,)), dma((2,)), dma, dma, dma((2, 8)), dma((2, 8)), dma((8,)), dma((8,)), dma((3,)), dma((3,)),
            dma((3,)), dma((3,)), dma, dma,
        ],
        compiler_params=pltpu.CompilerParams(
            collective_id=0, has_side_effects=True, vmem_limit_bytes=60 << 20
        ),
    )(distribution, pair_first, pair_second, pair_weight, proj_pair, proj_target, proj_coef, slot_counts)


def solution(mesh):
    in_specs = (
        P("vel", "cell"),
        P("vel", None, None),
        P("vel", None, None),
        P("vel", None, None),
        P("vel", None, None, None),
        P(None, None, "vel", None),
        P(None, None, "vel", None),
        P(None, None, "vel"),
    )
    out_specs = (P("vel", "cell"), P("vel", "cell"))
    return jax.shard_map(
        on_device, mesh=mesh, in_specs=in_specs, out_specs=out_specs, check_vma=False
    )
```

time: 105 us -> 79.6 us (0.76)
  the two profiles are of different devices: /device:TPU:16 before, /device:TPU:1 now
where the time goes in v2:
time: 79.6 us; the launch traced here: 79.5 us
  Pallas kernels  74.7 us (94%)
  local copies, waits for them, and re-layouts  4.14 us (5%)
    pallas_call x1, Pallas kernels, on_device(): pl.pallas_call(kernel, out_shape=(jax.ShapeDtypeStruct((ROWS, 128), F32),...  74.7 us
    unnamed x5, local copies, waits for them, and re-layouts  4.14 us

profile of v2, /device:TPU:1, one launch (start us, length us, event | category | flops | bytes accessed | tf_op | source)
XLA Modules:
  0.0 79.5 jit_solution(13088946033746945380)
XLA Ops:
  0.6 1.5 %copy.10.counts = s32[16,16,1]{2,1,0:T(8,128)} copy(s32[16,16,1]{1,2,0:T(1,128)} %param.15) | data formatting | bytes 2048 | tf_op args[7]
  2.1 74.7 %shard_map.95 = (f32[864,128]{1,0:T(8,128)}, f32[864,128]{1,0:T(8,128)}) custom-call(f32[864,128]{1,0:T(8,128)} %dist.1, s32[1,16,256]{2,1,0:T(8,128)} %first.1, s32[1,16,256]{2,1,0:T(8,128)} %second.1, f32[1,16,256]{2,1,0:T(8,128)} %weight.1, s32[1,16,16,64]{3,2,1,0:T(8,128)} %picks.1, s32[16,16,1,64]{3,2,1,0:T(1,128)} %target.1, f32[16,16,1,64]{3,2,1,0:T(1,128)} %coef.1, ...), custom_call_target="tpu_custom_call" | custom-call | tf_op jit(solution)/shard_map/pallas_call | solution.py:339
  76.8 0.0 copy-start
  76.8 1.9 %copy.13 = f32[864,128]{1,0:T(8,128)} copy(f32[864,128]{1,0:T(8,128)} %get-tuple-element.4) | data formatting | bytes 884736
  78.7 0.0 copy-done
  78.7 0.8 copy.14
Async XLA Ops:
  76.8 1.9 %copy-start = (f32[864,128]{1,0:T(8,128)S(1)}, f32[864,128]{1,0:T(8,128)}, u32[]{:S(2)}) copy-start(f32[864,128]{1,0:T(8,128)} %get-tuple-element.5) | copy-start | bytes 1327108

commit v3 on v2

--- a/solution.py
+++ b/solution.py
@@ -22,10 +22,10 @@
 
 
 def kernel(
-    dist, first, second, weight, picks, target, coef, counts,
-    out_t, out_c,
-    edge_out, edge_in, packed, ring, sends_idx, idx, pairs, args, wts, xs, ys, lossq, lossq_row, gain, loss, final,
-    edge_s, edge_r, part_s, part_r, ring_s, ring_r, zidx_s, zidx_r, xs_s, xs_r, cs_s, cs_r, fin_s, fin_r,
+    dist_hbm, first, second, weight, picks, target_hbm, coef_hbm, counts,
+    out_step, out_gain, out_loss,
+    dist, target, coef, columns, edge_out, edge_in, packed, ring, sends_idx, idx, pairs, args, wts, xs, ys, lossq, lossq_row, gain, loss, final, own,
+    edge_s, edge_r, part_s, part_r, ring_s, ring_r, zidx_s, zidx_r, xs_s, xs_r, cs_s, cs_r, fin_s, fin_r, local,
 ):
     vel = lax.axis_index("vel")
     cell = lax.axis_index("cell")
@@ -55,35 +55,21 @@
         copy.start()
         return copy
 
+    loads = [
+        pltpu.make_async_copy(src, dst, local.at[i])
+        for i, (src, dst) in enumerate(((dist_hbm, dist), (target_hbm, target), (coef_hbm, coef)))
+    ]
+    for load in loads:
+        load.start()
+
     lane8 = lax.broadcasted_iota(jnp.int32, (8, 128), 1)
     sub8 = lax.broadcasted_iota(jnp.int32, (8, 128), 0)
-    pick = jnp.where(lane8 == 127 * sub8, 1.0, 0.0).astype(F32)
-    edges = lax.dot_general(
-        pick, dist[...], (((1,), (1,)), ((), ())), precision=lax.Precision.HIGHEST, preferred_element_type=F32
-    )
-    edge_out[0] = edges[1:2]
-    edge_out[1] = edges[0:1]
-
-    for half in range(2):
-        rows = slice(half * 8, half * 8 + 8)
-        pairs[half, x, 0] = first[0, rows, :].astype(F32)
-        pairs[half, x, 1] = second[0, rows, :].astype(F32)
-        pairs[half, x, 2] = weight[0, rows, :]
-
-    pl.semaphore_wait(barrier, 10)
-
-    edge_copies = [
-        send(edge_out.at[0], edge_in.at[0], edge_s.at[0], edge_r.at[0], {"cell": right}),
-        send(edge_out.at[1], edge_in.at[1], edge_s.at[1], edge_r.at[1], {"cell": left}),
-    ]
-    pairs_copy = send(pairs.at[core, x], pairs.at[core, x], xs_s.at[0], xs_r.at[0], partner)
-
+    lane_first = lane8 < 64
     for b in range(8):
         groups = [2 * b + (half + x) % 2 for half in range(2)]
         take = jnp.concatenate([picks[0, group, pl.ds(core, 8, stride=2), :] for group in groups], axis=1)
         low = take & 127
         upper = take >= 128
-        lane_first = lane8 < 64
         for kind, table in enumerate((first, second, weight)):
             rows = []
             for group in groups:
@@ -95,31 +81,55 @@
                 lane_first, jnp.where(upper, rows[1], rows[0]), jnp.where(upper, rows[3], rows[2])
             ).astype(F32)
             for owner in range(8):
-                sends_idx[owner, pl.ds(kind * 8 + b, 1), :] = value[owner : owner + 1]
+                sends_idx[owner, kind * 8 + b : kind * 8 + b + 1, :] = value[owner : owner + 1]
+
+    pl.semaphore_wait(barrier, 10)
     z_copies = [
         send(sends_idx.at[(z + k) % 8], idx.at[core, x, z], zidx_s.at[k], zidx_r.at[k], at_z(k)) for k in range(1, 8)
     ]
     idx[core, x, pl.ds(z, 1)] = sends_idx[pl.ds(z, 1)]
 
-    for copy in edge_copies:
-        copy.wait_recv()
+    loads[0].wait()
+    pick = jnp.where(lane8 == 127 * sub8, 1.0, 0.0).astype(F32)
+    edges = lax.dot_general(
+        pick, dist[...], (((1,), (1,)), ((), ())), precision=lax.Precision.HIGHEST, preferred_element_type=F32
+    )
+    edge_out[0] = edges[1:2]
+    edge_out[1] = edges[0:1]
+    edge_copies = [
+        send(edge_out.at[0], edge_in.at[0], edge_s.at[0], edge_r.at[0], {"cell": right}),
+        send(edge_out.at[1], edge_in.at[1], edge_s.at[1], edge_r.at[1], {"cell": left}),
+    ]
+
+    for half in range(2):
+        rows = slice(half * 8, half * 8 + 8)
+        pairs[half, x, 0] = first[0, rows, :].astype(F32)
+        pairs[half, x, 1] = second[0, rows, :].astype(F32)
+        pairs[half, x, 2] = weight[0, rows, :]
+    pairs_copy = send(pairs.at[core, x], pairs.at[core, x], xs_s.at[0], xs_r.at[0], partner)
+
     node = vel * ROWS + lax.broadcasted_iota(jnp.int32, (ROWS, 128), 0)
     courant = (2 * (node // (VSIDE * VSIDE)) - VSIDE + 1).astype(F32) / (2.0 * VSIDE)
     lane = lax.broadcasted_iota(jnp.int32, (ROWS, 128), 1)
     here = dist[...]
+    for copy in z_copies:
+        copy.wait_recv()
+    idx_copy = send(idx.at[core, x], idx.at[core, x], xs_s.at[2], xs_r.at[2], partner)
+    for copy in edge_copies:
+        copy.wait_recv()
 
     def column(row):
         return jnp.broadcast_to(row, (8, ROWS)).T[:, 0:1]
 
     before = jnp.where(lane == 0, column(edge_in[0]), pltpu.roll(here, 1, axis=1))
     after = jnp.where(lane == 127, column(edge_in[1]), pltpu.roll(here, 127, axis=1))
-    moved = here - jnp.maximum(courant, 0.0) * (here - before) - jnp.minimum(courant, 0.0) * (after - here)
-    out_t[...] = moved
+    change = jnp.maximum(courant, 0.0) * (here - before) + jnp.minimum(courant, 0.0) * (after - here)
+    moved = here - change
+    out_step[...] = change
     top, low = moved[:HALF], moved[HALF:]
     lane_low = lax.broadcasted_iota(jnp.int32, (HALF, 128), 1) < 64
     packed[0] = jnp.where(lane_low, top, pltpu.roll(low, 64, axis=1))
     packed[1] = jnp.where(lane_low, pltpu.roll(top, 64, axis=1), low)
-    ring[0, pl.ds(x, 1)] = packed[pl.ds(x, 1)]
 
     def ring_copy(way, step, src_m, dst_m, group):
         return pltpu.make_async_remote_copy(
@@ -131,46 +141,48 @@
             device_id_type=MESH,
         )
 
+    ring[0, pl.ds(x, 1)] = packed[pl.ds(x, 1)]
     ring_copy(0, 1, 0, 1, x).start()
     ring_copy(1, 1, 0, 2, x).start()
     part_copy = send(packed.at[y], ring.at[0, x], part_s, part_r, partner)
 
+    gain[...] = jnp.zeros_like(gain)
+    loss[...] = jnp.zeros_like(loss)
+    wts[...] = jnp.zeros_like(wts)
+    idx_copy.wait_recv()
+    idx_on = send(idx.at[core], idx.at[core], cs_s.at[2], cs_r.at[2], sibling)
+    pairs_copy.wait_recv()
+    pairs_on = send(pairs.at[core, y], pairs.at[core, y], cs_s.at[0], cs_r.at[0], sibling)
+
+    loads[1].wait()
+    loads[2].wait()
+    columns[:, 0:16] = counts[:, 0, :].T
+    live = [columns[pl.ds(tile, 8, stride=2), :] for tile in range(2)]
     slot = lax.broadcasted_iota(jnp.int32, (8, 64), 1)
-    for s in range(16):
-        rows = []
-        for half in range(2):
-            every = pl.ds((half + s) % 2, 8, stride=2)
-            rows.append(jnp.where(slot < counts[s, every, :], coef[s, every, 0, :], 0.0))
-        args[0, x, s * 8 : s * 8 + 8] = jnp.concatenate(rows, axis=1)
     for a in range(8):
         for tile in range(2):
             every = pl.ds(tile, 8, stride=2)
-            rows = [target[2 * a + (half + tile) % 2, every, 0, :] for half in range(2)]
+            sources = [2 * a + (half + tile) % 2 for half in range(2)]
             start = a * 16 + tile * 8
-            args[1, x, start : start + 8] = jnp.concatenate(rows, axis=1).astype(F32)
+            args[0, x, start : start + 8] = jnp.concatenate(
+                [jnp.where(slot < live[tile][:, s : s + 1], coef[s, every, 0, :], 0.0) for s in sources], axis=1
+            )
+            args[1, x, start : start + 8] = jnp.concatenate(
+                [target[s, every, 0, :] for s in sources], axis=1
+            ).astype(F32)
     args_copy = send(args.at[core, x], args.at[core, x], xs_s.at[1], xs_r.at[1], partner)
-
-    for copy in z_copies:
-        copy.wait_recv()
-    idx_copy = send(idx.at[core, x], idx.at[core, x], xs_s.at[2], xs_r.at[2], partner)
-
-    gain[...] = jnp.zeros_like(gain)
-    loss[...] = jnp.zeros_like(loss)
-    wts[...] = jnp.zeros_like(wts)
 
     part_copy.wait_recv()
     ring_copy(0, 2, 0, 1, y).start()
     ring_copy(1, 2, 0, 2, y).start()
-
-    pairs_copy.wait_recv()
-    pairs_on = send(pairs.at[core, y], pairs.at[core, y], cs_s.at[0], cs_r.at[0], sibling)
-    args_copy.wait_recv()
-    args_on = send(args.at[core, y], args.at[core, y], cs_s.at[1], cs_r.at[1], sibling)
-    idx_copy.wait_recv()
-    idx_on = send(idx.at[core], idx.at[core], cs_s.at[2], cs_r.at[2], sibling)
     pairs_on.wait_recv()
-    args_on.wait_recv()
     idx_on.wait_recv()
+
+    def args_on():
+        return pltpu.make_async_remote_copy(
+            src_ref=args.at[core, y], dst_ref=args.at[core, y], send_sem=cs_s.at[1], recv_sem=cs_r.at[1],
+            device_id=sibling, device_id_type=MESH,
+        )
 
     def place(m):
         return (z + (m % 2) * (8 - (m + 1) // 2) + (1 - m % 2) * (m // 2)) % 8
@@ -200,7 +212,7 @@
         found = found[0:128] + found[128:256]
         found = jnp.where(upper, found[64:128], found[0:64])
         for b in range(8):
-            scale = idx[e, group, zz, 16 + b : 17 + b, :] * args[0, e, pl.ds(actual * 8 + b, 1), :]
+            scale = idx[e, group, zz, 16 + b : 17 + b, :]
             xs[m, group, e, b] = found[:, b * 128 : b * 128 + 128] * scale
             ys[m, group, e, b] = found[:, 1024 + b * 128 : 1024 + b * 128 + 128]
         share = pairs[pair_half, e, 2, pair_row, :]
@@ -236,17 +248,19 @@
             even, odd = xs[ma, 0, e, zb], xs[ma, 1, e, zb]
             for tile in range(2):
                 mine = jnp.where(tile_low, even, odd) if tile == 0 else jnp.where(tile_low, odd, even)
-                goal = args[1, e, pl.ds(za * 16 + tile * 8 + zb, 1), :]
+                row = pl.ds(za * 16 + tile * 8 + zb, 1)
+                goal = args[1, e, row, :]
                 upper = goal >= float(HALF)
-                terms.append(split_terms(mine * ys[mb, tile, e, za], upper))
+                terms.append(split_terms(mine * ys[mb, tile, e, za] * args[0, e, row, :], upper))
                 goals.append(jnp.where(upper, goal - float(HALF), goal))
         gain[e] += scatter(goals, terms)
         return e
 
-    def finish(e):
+    def finish(e, where):
         g = gain[e]
         s = loss[e]
-        return g[:, 0:128] + g[:, 128:256] - ring[0, e] * (s[:, 0:128] + s[:, 128:256])
+        where[0] = g[:, 0:128] + g[:, 128:256]
+        where[1] = ring[0, e] * (s[:, 0:128] + s[:, 128:256])
 
     def final_copy():
         return pltpu.make_async_remote_copy(
@@ -276,6 +290,15 @@
         @pl.when((t >= 5) & (t <= 6))
         def _():
             ring_copy(group, 7, 5 + group, 7, group).start()
+
+        @pl.when(t == 1)
+        def _():
+            args_copy.wait_recv()
+            args_on().start()
+
+        @pl.when(t == 2)
+        def _():
+            args_on().wait_recv()
 
         ends = last + (7 - t) // 7
         arrived = []
@@ -305,7 +328,8 @@
 
             @pl.when((t == 7) & (turn == 0))
             def _():
-                packed[0] = finish(y)
+                finish(y, packed)
+                packed[0] = packed[0] - packed[1]
                 final_copy().start()
 
             return inner
@@ -315,14 +339,20 @@
 
     lax.fori_loop(0, 8, step, 0)
 
-    final[pl.ds(x, 1)] = finish(x)[None]
+    finish(x, own)
     final_copy().wait_recv()
-    lo, hi = final[0], final[1]
-    out_c[0:HALF, :] = jnp.where(lane_low, lo, pltpu.roll(hi, 64, axis=1))
-    out_c[HALF:ROWS, :] = jnp.where(lane_low, pltpu.roll(lo, 64, axis=1), hi)
+
+    def unpacked(mine, theirs, ref):
+        lo = jnp.where(x == 0, mine, theirs)
+        hi = jnp.where(x == 0, theirs, mine)
+        ref[0:HALF, :] = jnp.where(lane_low, lo, pltpu.roll(hi, 64, axis=1))
+        ref[HALF:ROWS, :] = jnp.where(lane_low, pltpu.roll(lo, 64, axis=1), hi)
+
+    unpacked(own[0], final[y], out_gain)
+    unpacked(own[1], jnp.zeros((HALF, 128), F32), out_loss)
 
     final_copy().wait_send()
-    for copy in edge_copies + z_copies + [pairs_copy, args_copy, idx_copy, pairs_on, args_on, idx_on]:
+    for copy in edge_copies + z_copies + [pairs_copy, args_copy, idx_copy, pairs_on, args_on(), idx_on]:
         copy.wait_send()
 
     def drain(t, carry):
@@ -335,13 +365,19 @@
 
 def on_device(distribution, pair_first, pair_second, pair_weight, proj_pair, proj_target, proj_coef, slot_counts):
     vmem = pl.BlockSpec(memory_space=pltpu.VMEM)
+    hbm = pl.BlockSpec(memory_space=pl.ANY)
     dma = pltpu.SemaphoreType.DMA
-    return pl.pallas_call(
+    block = jax.ShapeDtypeStruct((ROWS, 128), F32)
+    change, gain, loss = pl.pallas_call(
         kernel,
-        out_shape=(jax.ShapeDtypeStruct((ROWS, 128), F32), jax.ShapeDtypeStruct((ROWS, 128), F32)),
-        in_specs=[vmem] * 8,
-        out_specs=(vmem, vmem),
+        out_shape=(block, block, block),
+        in_specs=[hbm, vmem, vmem, vmem, vmem, hbm, hbm, vmem],
+        out_specs=(vmem, vmem, vmem),
         scratch_shapes=[
+            pltpu.VMEM((ROWS, 128), F32),
+            pltpu.VMEM((16, 16, 1, 64), jnp.int32),
+            pltpu.VMEM((16, 16, 1, 64), F32),
+            pltpu.VMEM((16, 128), jnp.int32),
             pltpu.VMEM((2, 1, ROWS), F32),
             pltpu.VMEM((2, 1, ROWS), F32),
             pltpu.VMEM((2, HALF, 128), F32),
@@ -358,13 +394,19 @@
             pltpu.VMEM((2, HALF, 256), F32),
             pltpu.VMEM((2, HALF, 256), F32),
             pltpu.VMEM((2, HALF, 128), F32),
+            pltpu.VMEM((2, HALF, 128), F32),
             dma((2,)), dma((2,)), dma, dma, dma((2, 8)), dma((2, 8)), dma((8,)), dma((8,)), dma((3,)), dma((3,)),
             dma((3,)), dma((3,)), dma, dma,
+            dma((3,)),
         ],
         compiler_params=pltpu.CompilerParams(
             collective_id=0, has_side_effects=True, vmem_limit_bytes=60 << 20
         ),
-    )(distribution, pair_first, pair_second, pair_weight, proj_pair, proj_target, proj_coef, slot_counts)
+    )(
+        distribution, pair_first, pair_second, pair_weight, proj_pair, proj_target, proj_coef,
+        slot_counts.transpose(0, 2, 1),
+    )
+    return distribution - change, gain - loss
 
 
 def solution(mesh):

time: 79.6 us -> 74.7 us (0.938)
  the two profiles are of different devices: /device:TPU:1 before, /device:TPU:16 now
where the time goes in v3:
time: 74.7 us; the launch traced here: 74.2 us
  Pallas kernels  70.8 us (95%)
  other arithmetic  2.71 us (4%)
    pallas_call x1, Pallas kernels, on_device(): pl.pallas_call(kernel, out_shape=(block, block, block), in_specs=[hbm, vm...  70.8 us
    sub x2, other arithmetic, on_device(): return (distribution - change, gain - loss)  2.71 us

profile of v3, /device:TPU:16, one launch (start us, length us, event | category | flops | bytes accessed | tf_op | source)
XLA Modules:
  0.0 74.2 jit_solution(12221332930741836503)
XLA Ops:
  0.6 0.0 copy-start
  0.6 70.8 %shard_map.95 = (f32[864,128]{1,0:T(8,128)}, f32[864,128]{1,0:T(8,128)}, f32[864,128]{1,0:T(8,128)}) custom-call(f32[864,128]{1,0:T(8,128)} %dist_hbm.1, s32[1,16,256]{2,1,0:T(8,128)} %first.1, s32[1,16,256]{2,1,0:T(8,128)} %second.1, f32[1,16,256]{2,1,0:T(8,128)} %weight.1, s32[1,16,16,64]{3,2,1,0:T(8,128)} %picks.1, s32[16,16,1,64]{3,2,1,0:T(1,128)} %target_hbm.1, ...), custom_call_target="tpu_custom_call" | custom-call | tf_op jit(solution)/shard_map/pallas_call | solution.py:371
  71.5 0.0 copy-done
  71.5 0.0 copy-start.1
  71.5 0.0 copy-start.2
  71.5 1.9 %sub.6 = f32[864,128]{1,0:T(8,128)} subtract(f32[864,128]{1,0:T(8,128)S(1)} %copy-done, f32[864,128]{1,0:T(8,128)} %get-tuple-element.5) | non-fusion elementwise | flops 110592 | bytes 1327104 | tf_op jit(solution)/shard_map/sub | solution.py:409
  73.4 0.0 copy-done.1
  73.4 0.0 copy-done.2
  73.4 0.8 %sub.7 = f32[864,128]{1,0:T(8,128)} subtract(f32[864,128]{1,0:T(8,128)S(1)} %copy-done.1, f32[864,128]{1,0:T(8,128)S(1)} %copy-done.2) | non-fusion elementwise | flops 110592 | bytes 1327104 | tf_op jit(solution)/shard_map/sub | solution.py:409
Async XLA Ops:
  0.6 70.8 %copy-start = (f32[864,128]{1,0:T(8,128)S(1)}, f32[864,128]{1,0:T(8,128)}, u32[]{:S(2)}) copy-start(f32[864,128]{1,0:T(8,128)} %dist_hbm.1) | copy-start | bytes 1327108
  71.5 1.9 %copy-start.1 = (f32[864,128]{1,0:T(8,128)S(1)}, f32[864,128]{1,0:T(8,128)}, u32[]{:S(2)}) copy-start(f32[864,128]{1,0:T(8,128)} %get-tuple-element.6) | copy-start | bytes 1327108
  71.5 1.9 %copy-start.2 = (f32[864,128]{1,0:T(8,128)S(1)}, f32[864,128]{1,0:T(8,128)}, u32[]{:S(2)}) copy-start(f32[864,128]{1,0:T(8,128)} %get-tuple-element.7) | copy-start | bytes 1327108

commit v4 on v3

--- a/solution.py
+++ b/solution.py
@@ -22,10 +22,11 @@
 
 
 def kernel(
-    dist_hbm, first, second, weight, picks, target_hbm, coef_hbm, counts,
+    dist_hbm, first_hbm, second_hbm, weight_hbm, picks_hbm, target_hbm, coef_hbm, counts_hbm,
     out_step, out_gain, out_loss,
-    dist, target, coef, columns, edge_out, edge_in, packed, ring, sends_idx, idx, pairs, args, wts, xs, ys, lossq, lossq_row, gain, loss, final, own,
-    edge_s, edge_r, part_s, part_r, ring_s, ring_r, zidx_s, zidx_r, xs_s, xs_r, cs_s, cs_r, fin_s, fin_r, local,
+    dist, target, coef, first, second, weight, picks, counts,
+    columns, edge_out, edge_in, edge_row, ring_edge, packed, ring, sends_idx, idx, pairs, args, wts, xs, ys, lossq, lossq_row, gain, loss, final, own,
+    edge_s, edge_r, part_s, part_r, ring_s, ring_r, zidx_s, zidx_r, xs_s, xs_r, cs_s, cs_r, fin_s, fin_r, local, redge_s, redge_r, pedge_s, pedge_r,
 ):
     vel = lax.axis_index("vel")
     cell = lax.axis_index("cell")
@@ -57,10 +58,17 @@
 
     loads = [
         pltpu.make_async_copy(src, dst, local.at[i])
-        for i, (src, dst) in enumerate(((dist_hbm, dist), (target_hbm, target), (coef_hbm, coef)))
+        for i, (src, dst) in enumerate(
+            (
+                (picks_hbm, picks), (first_hbm, first), (second_hbm, second), (weight_hbm, weight), (dist_hbm, dist),
+                (counts_hbm, counts), (target_hbm, target), (coef_hbm, coef),
+            )
+        )
     ]
     for load in loads:
         load.start()
+    for load in loads[:4]:
+        load.wait()
 
     lane8 = lax.broadcasted_iota(jnp.int32, (8, 128), 1)
     sub8 = lax.broadcasted_iota(jnp.int32, (8, 128), 0)
@@ -83,53 +91,25 @@
             for owner in range(8):
                 sends_idx[owner, kind * 8 + b : kind * 8 + b + 1, :] = value[owner : owner + 1]
 
+    loads[4].wait()
+    node = vel * ROWS + lax.broadcasted_iota(jnp.int32, (ROWS, 128), 0)
+    courant = (2 * (node // (VSIDE * VSIDE)) - VSIDE + 1).astype(F32) / (2.0 * VSIDE)
+    positive, negative = jnp.maximum(courant, 0.0), jnp.minimum(courant, 0.0)
+    lane = lax.broadcasted_iota(jnp.int32, (ROWS, 128), 1)
+    lane_low = lax.broadcasted_iota(jnp.int32, (HALF, 128), 1) < 64
+    here = dist[...]
+    moved = here - (
+        positive * (here - pltpu.roll(here, 1, axis=1)) + negative * (pltpu.roll(here, 127, axis=1) - here)
+    )
+    top, low = moved[:HALF], moved[HALF:]
+    packed[0] = jnp.where(lane_low, top, pltpu.roll(low, 64, axis=1))
+    packed[1] = jnp.where(lane_low, pltpu.roll(top, 64, axis=1), low)
+    ring[0, pl.ds(x, 1)] = packed[pl.ds(x, 1)]
+
     pl.semaphore_wait(barrier, 10)
     z_copies = [
         send(sends_idx.at[(z + k) % 8], idx.at[core, x, z], zidx_s.at[k], zidx_r.at[k], at_z(k)) for k in range(1, 8)
     ]
-    idx[core, x, pl.ds(z, 1)] = sends_idx[pl.ds(z, 1)]
-
-    loads[0].wait()
-    pick = jnp.where(lane8 == 127 * sub8, 1.0, 0.0).astype(F32)
-    edges = lax.dot_general(
-        pick, dist[...], (((1,), (1,)), ((), ())), precision=lax.Precision.HIGHEST, preferred_element_type=F32
-    )
-    edge_out[0] = edges[1:2]
-    edge_out[1] = edges[0:1]
-    edge_copies = [
-        send(edge_out.at[0], edge_in.at[0], edge_s.at[0], edge_r.at[0], {"cell": right}),
-        send(edge_out.at[1], edge_in.at[1], edge_s.at[1], edge_r.at[1], {"cell": left}),
-    ]
-
-    for half in range(2):
-        rows = slice(half * 8, half * 8 + 8)
-        pairs[half, x, 0] = first[0, rows, :].astype(F32)
-        pairs[half, x, 1] = second[0, rows, :].astype(F32)
-        pairs[half, x, 2] = weight[0, rows, :]
-    pairs_copy = send(pairs.at[core, x], pairs.at[core, x], xs_s.at[0], xs_r.at[0], partner)
-
-    node = vel * ROWS + lax.broadcasted_iota(jnp.int32, (ROWS, 128), 0)
-    courant = (2 * (node // (VSIDE * VSIDE)) - VSIDE + 1).astype(F32) / (2.0 * VSIDE)
-    lane = lax.broadcasted_iota(jnp.int32, (ROWS, 128), 1)
-    here = dist[...]
-    for copy in z_copies:
-        copy.wait_recv()
-    idx_copy = send(idx.at[core, x], idx.at[core, x], xs_s.at[2], xs_r.at[2], partner)
-    for copy in edge_copies:
-        copy.wait_recv()
-
-    def column(row):
-        return jnp.broadcast_to(row, (8, ROWS)).T[:, 0:1]
-
-    before = jnp.where(lane == 0, column(edge_in[0]), pltpu.roll(here, 1, axis=1))
-    after = jnp.where(lane == 127, column(edge_in[1]), pltpu.roll(here, 127, axis=1))
-    change = jnp.maximum(courant, 0.0) * (here - before) + jnp.minimum(courant, 0.0) * (after - here)
-    moved = here - change
-    out_step[...] = change
-    top, low = moved[:HALF], moved[HALF:]
-    lane_low = lax.broadcasted_iota(jnp.int32, (HALF, 128), 1) < 64
-    packed[0] = jnp.where(lane_low, top, pltpu.roll(low, 64, axis=1))
-    packed[1] = jnp.where(lane_low, pltpu.roll(top, 64, axis=1), low)
 
     def ring_copy(way, step, src_m, dst_m, group):
         return pltpu.make_async_remote_copy(
@@ -141,10 +121,74 @@
             device_id_type=MESH,
         )
 
-    ring[0, pl.ds(x, 1)] = packed[pl.ds(x, 1)]
+    def edge_copy(way, step, src_m, dst_m, group):
+        return pltpu.make_async_remote_copy(
+            src_ref=ring_edge.at[src_m, group],
+            dst_ref=ring_edge.at[dst_m, group],
+            send_sem=redge_s.at[way, step],
+            recv_sem=redge_r.at[way, step],
+            device_id=at_z(1 - 2 * way),
+            device_id_type=MESH,
+        )
+
     ring_copy(0, 1, 0, 1, x).start()
     ring_copy(1, 1, 0, 2, x).start()
     part_copy = send(packed.at[y], ring.at[0, x], part_s, part_r, partner)
+    idx[core, x, pl.ds(z, 1)] = sends_idx[pl.ds(z, 1)]
+
+    pick = jnp.where(lane8 == sub8 + jnp.where(sub8 < 2, 0, 124), 1.0, 0.0).astype(F32)
+    pick = jnp.where(sub8 < 4, pick, 0.0)
+    halves = [
+        lax.dot_general(
+            pick, dist[part * HALF : part * HALF + HALF, :], (((1,), (1,)), ((), ())),
+            precision=lax.Precision.HIGHEST, preferred_element_type=F32,
+        )
+        for part in range(2)
+    ]
+    near = [jnp.concatenate([half[i : i + 1] for half in halves], axis=0) for i in range(4)]
+    edge_out[0] = near[3]
+    edge_out[1] = near[0]
+    edge_copies = [
+        send(edge_out.at[0], edge_in.at[0], edge_s.at[0], edge_r.at[0], {"cell": right}),
+        send(edge_out.at[1], edge_in.at[1], edge_s.at[1], edge_r.at[1], {"cell": left}),
+    ]
+
+    for half in range(2):
+        rows = slice(half * 8, half * 8 + 8)
+        pairs[half, x, 0] = first[0, rows, :].astype(F32)
+        pairs[half, x, 1] = second[0, rows, :].astype(F32)
+        pairs[half, x, 2] = weight[0, rows, :]
+    pairs_copy = send(pairs.at[core, x], pairs.at[core, x], xs_s.at[0], xs_r.at[0], partner)
+
+    for copy in z_copies:
+        copy.wait_recv()
+    idx_copy = send(idx.at[core, x], idx.at[core, x], xs_s.at[2], xs_r.at[2], partner)
+
+    for copy in edge_copies:
+        copy.wait_recv()
+    row_node = (
+        vel * ROWS
+        + lax.broadcasted_iota(jnp.int32, (2, HALF), 0) * HALF
+        + lax.broadcasted_iota(jnp.int32, (2, HALF), 1)
+    )
+    row_courant = (2 * (row_node // (VSIDE * VSIDE)) - VSIDE + 1).astype(F32) / (2.0 * VSIDE)
+    row_positive, row_negative = jnp.maximum(row_courant, 0.0), jnp.minimum(row_courant, 0.0)
+    edge_row[0] = near[0] - (row_positive * (near[0] - edge_in[0]) + row_negative * (near[1] - near[0]))
+    edge_row[1] = near[3] - (row_positive * (near[3] - near[2]) + row_negative * (edge_in[1] - near[3]))
+    ring_edge[0, pl.ds(x, 1)] = edge_row[pl.ds(x, 1)]
+    edge_copy(0, 1, 0, 1, x).start()
+    edge_copy(1, 1, 0, 2, x).start()
+    pedge_copy = send(edge_row.at[y], ring_edge.at[0, x], pedge_s, pedge_r, partner)
+
+    def column(rows):
+        return jnp.broadcast_to(rows, (8, HALF)).T[:, 0:1]
+
+    def full_column(rows):
+        return jnp.concatenate([column(rows[0:1]), column(rows[1:2])], axis=0)
+
+    before = jnp.where(lane == 0, full_column(edge_in[0]), pltpu.roll(here, 1, axis=1))
+    after = jnp.where(lane == 127, full_column(edge_in[1]), pltpu.roll(here, 127, axis=1))
+    out_step[...] = positive * (here - before) + negative * (after - here)
 
     gain[...] = jnp.zeros_like(gain)
     loss[...] = jnp.zeros_like(loss)
@@ -154,8 +198,8 @@
     pairs_copy.wait_recv()
     pairs_on = send(pairs.at[core, y], pairs.at[core, y], cs_s.at[0], cs_r.at[0], sibling)
 
-    loads[1].wait()
-    loads[2].wait()
+    for load in loads[5:]:
+        load.wait()
     columns[:, 0:16] = counts[:, 0, :].T
     live = [columns[pl.ds(tile, 8, stride=2), :] for tile in range(2)]
     slot = lax.broadcasted_iota(jnp.int32, (8, 64), 1)
@@ -175,6 +219,9 @@
     part_copy.wait_recv()
     ring_copy(0, 2, 0, 1, y).start()
     ring_copy(1, 2, 0, 2, y).start()
+    pedge_copy.wait_recv()
+    edge_copy(0, 2, 0, 1, y).start()
+    edge_copy(1, 2, 0, 2, y).start()
     pairs_on.wait_recv()
     idx_on.wait_recv()
 
@@ -260,7 +307,10 @@
         g = gain[e]
         s = loss[e]
         where[0] = g[:, 0:128] + g[:, 128:256]
-        where[1] = ring[0, e] * (s[:, 0:128] + s[:, 128:256])
+        lanes = lax.broadcasted_iota(jnp.int32, (HALF, 128), 1)
+        value = jnp.where(lanes == 63 * x, column(ring_edge[0, e, 0:1, :]), ring[0, e])
+        value = jnp.where(lanes == 63 * x + 64, column(ring_edge[0, e, 1:2, :]), value)
+        where[1] = value * (s[:, 0:128] + s[:, 128:256])
 
     def final_copy():
         return pltpu.make_async_remote_copy(
@@ -268,6 +318,7 @@
             device_id_type=MESH,
         )
 
+    cell_row = lax.broadcasted_iota(jnp.int32, (128, HALF), 0)
     part_copy.wait_send()
 
     def step(t, carry):
@@ -281,15 +332,20 @@
             m1 = 2 * k - last
             ring_copy(0, t, m0, m0, (1 - last) * group).wait_recv()
             ring_copy(1, t, m1, m1, (1 - last) * group + last).wait_recv()
+            edge_copy(0, t, m0, m0, (1 - last) * group).wait_recv()
+            edge_copy(1, t, m1, m1, (1 - last) * group + last).wait_recv()
 
         @pl.when((t >= 1) & (t <= 4))
         def _():
             ring_copy(0, t + 2, 2 * k - 1, 2 * k + 1, group).start()
             ring_copy(1, t + 2, 2 * k, 2 * k + 2, group).start()
+            edge_copy(0, t + 2, 2 * k - 1, 2 * k + 1, group).start()
+            edge_copy(1, t + 2, 2 * k, 2 * k + 2, group).start()
 
         @pl.when((t >= 5) & (t <= 6))
         def _():
             ring_copy(group, 7, 5 + group, 7, group).start()
+            edge_copy(group, 7, 5 + group, 7, group).start()
 
         @pl.when(t == 1)
         def _():
@@ -306,7 +362,10 @@
             m = (1 - ends) * (2 * k - 1 + i) + last * 7
             g = (1 - ends) * group + ends * i
             arrived.append((m, g))
-            high, rest = split(ring[m, g].T)
+            turned = ring[m, g].T
+            turned = jnp.where(cell_row == 63 * x, ring_edge[m, g, 0:1, :], turned)
+            turned = jnp.where(cell_row == 63 * x + 64, ring_edge[m, g, 1:2, :], turned)
+            high, rest = split(turned)
             wts[i, 0:128, 0:HALF] = high
             wts[i, 128:256, 0:HALF] = rest
 
@@ -352,12 +411,14 @@
     unpacked(own[1], jnp.zeros((HALF, 128), F32), out_loss)
 
     final_copy().wait_send()
-    for copy in edge_copies + z_copies + [pairs_copy, args_copy, idx_copy, pairs_on, args_on(), idx_on]:
+    for copy in edge_copies + z_copies + [pairs_copy, args_copy, idx_copy, pairs_on, args_on(), idx_on, pedge_copy]:
         copy.wait_send()
 
     def drain(t, carry):
         ring_copy(0, t, 0, 0, 0).wait_send()
         ring_copy(1, t, 0, 0, 0).wait_send()
+        edge_copy(0, t, 0, 0, 0).wait_send()
+        edge_copy(1, t, 0, 0, 0).wait_send()
         return carry
 
     lax.fori_loop(1, 8, drain, 0)
@@ -365,21 +426,28 @@
 
 def on_device(distribution, pair_first, pair_second, pair_weight, proj_pair, proj_target, proj_coef, slot_counts):
     vmem = pl.BlockSpec(memory_space=pltpu.VMEM)
-    hbm = pl.BlockSpec(memory_space=pl.ANY)
+    hbm = pl.BlockSpec(memory_space=pltpu.HBM)
     dma = pltpu.SemaphoreType.DMA
     block = jax.ShapeDtypeStruct((ROWS, 128), F32)
     change, gain, loss = pl.pallas_call(
         kernel,
         out_shape=(block, block, block),
-        in_specs=[hbm, vmem, vmem, vmem, vmem, hbm, hbm, vmem],
+        in_specs=[hbm] * 8,
         out_specs=(vmem, vmem, vmem),
         scratch_shapes=[
             pltpu.VMEM((ROWS, 128), F32),
             pltpu.VMEM((16, 16, 1, 64), jnp.int32),
             pltpu.VMEM((16, 16, 1, 64), F32),
+            pltpu.VMEM((1, 16, 256), jnp.int32),
+            pltpu.VMEM((1, 16, 256), jnp.int32),
+            pltpu.VMEM((1, 16, 256), F32),
+            pltpu.VMEM((1, 16, 16, 64), jnp.int32),
+            pltpu.VMEM((16, 1, 16), jnp.int32),
             pltpu.VMEM((16, 128), jnp.int32),
-            pltpu.VMEM((2, 1, ROWS), F32),
-            pltpu.VMEM((2, 1, ROWS), F32),
+            pltpu.VMEM((2, 2, HALF), F32),
+            pltpu.VMEM((2, 2, HALF), F32),
+            pltpu.VMEM((2, 2, HALF), F32),
+            pltpu.VMEM((8, 2, 2, HALF), F32),
             pltpu.VMEM((2, HALF, 128), F32),
             pltpu.VMEM((8, 2, HALF, 128), F32),
             pltpu.VMEM((8, 24, 128), F32),
@@ -397,7 +465,7 @@
             pltpu.VMEM((2, HALF, 128), F32),
             dma((2,)), dma((2,)), dma, dma, dma((2, 8)), dma((2, 8)), dma((8,)), dma((8,)), dma((3,)), dma((3,)),
             dma((3,)), dma((3,)), dma, dma,
-            dma((3,)),
+            dma((8,)), dma((2, 8)), dma((2, 8)), dma, dma,
         ],
         compiler_params=pltpu.CompilerParams(
             collective_id=0, has_side_effects=True, vmem_limit_bytes=60 << 20

time: 74.7 us -> 74.3 us (level)
  no operation moved by 1% of the time
where the time goes in v4:
time: 74.3 us; the launch traced here: 73.8 us
  Pallas kernels  70.4 us (95%)
  other arithmetic  2.71 us (4%)
    pallas_call x1, Pallas kernels, on_device(): pl.pallas_call(kernel, out_shape=(block, block, block), in_specs=[hbm] *...  70.4 us
    sub x2, other arithmetic, on_device(): return (distribution - change, gain - loss)  2.71 us

profile of v4, /device:TPU:16, one launch (start us, length us, event | category | flops | bytes accessed | tf_op | source)
XLA Modules:
  0.0 73.8 jit_solution(9678901883979452802)
XLA Ops:
  0.6 0.0 copy-start
  0.6 70.4 %shard_map.95 = (f32[864,128]{1,0:T(8,128)}, f32[864,128]{1,0:T(8,128)}, f32[864,128]{1,0:T(8,128)}) custom-call(f32[864,128]{1,0:T(8,128)} %dist_hbm.1, s32[1,16,256]{2,1,0:T(8,128)} %first_hbm.1, s32[1,16,256]{2,1,0:T(8,128)} %second_hbm.1, f32[1,16,256]{2,1,0:T(8,128)} %weight_hbm.1, s32[1,16,16,64]{3,2,1,0:T(8,128)} %picks_hbm.1, ...), custom_call_target="tpu_custom_call" | custom-call | tf_op jit(solution)/shard_map/pallas_call | solution.py:432
  71.1 0.0 copy-done
  71.1 0.0 copy-start.1
  71.1 0.0 copy-start.2
  71.1 1.9 %sub.6 = f32[864,128]{1,0:T(8,128)} subtract(f32[864,128]{1,0:T(8,128)S(1)} %copy-done, f32[864,128]{1,0:T(8,128)} %get-tuple-element.5) | non-fusion elementwise | flops 110592 | bytes 1327104 | tf_op jit(solution)/shard_map/sub | solution.py:477
  73.0 0.0 copy-done.1
  73.0 0.0 copy-done.2
  73.0 0.8 %sub.7 = f32[864,128]{1,0:T(8,128)} subtract(f32[864,128]{1,0:T(8,128)S(1)} %copy-done.1, f32[864,128]{1,0:T(8,128)S(1)} %copy-done.2) | non-fusion elementwise | flops 110592 | bytes 1327104 | tf_op jit(solution)/shard_map/sub | solution.py:477
Async XLA Ops:
  0.6 70.4 %copy-start = (f32[864,128]{1,0:T(8,128)S(1)}, f32[864,128]{1,0:T(8,128)}, u32[]{:S(2)}) copy-start(f32[864,128]{1,0:T(8,128)} %dist_hbm.1) | copy-start | bytes 1327108
  71.1 1.9 %copy-start.1 = (f32[864,128]{1,0:T(8,128)S(1)}, f32[864,128]{1,0:T(8,128)}, u32[]{:S(2)}) copy-start(f32[864,128]{1,0:T(8,128)} %get-tuple-element.6) | copy-start | bytes 1327108
  71.1 1.9 %copy-start.2 = (f32[864,128]{1,0:T(8,128)S(1)}, f32[864,128]{1,0:T(8,128)}, u32[]{:S(2)}) copy-start(f32[864,128]{1,0:T(8,128)} %get-tuple-element.7) | copy-start | bytes 1327108
